TPU v7x, 32 devices: a whole 2x2x4 slice. The times are simulated.
32 devices in a mesh: ctx: 8 (over z, x), kvh: 4 (over y, core).
Axes of the slice: x: 2, y: 2, z: 4, core: 2. Of those that a mesh axis runs over, the one named last changes fastest.
Arguments:
- queries: bfloat16 [12, 16, 8192], P(None, None, 'kvh'), may hold values from -100 to 100
- keys: bfloat16 [512, 8, 256, 128], P('ctx', 'kvh'), may hold values from -8 to 8
- values: bfloat16 [512, 8, 256, 128], P('ctx', 'kvh'), may hold values from -6 to 6
- out_weight: bfloat16 [8192, 8192], P('kvh', 'ctx'), may hold values from -0.0625 to 0.0625
- lengths: int32 [12], replicated, may hold values from 16 to 16384, as said below
- slot_request: int32 [512], P('ctx'), may hold values from 0 to 12, as said below
- slot_page: int32 [512], P('ctx'), may hold values from 0 to 63, as said below
Outputs:
- projected: bfloat16 [192, 8192], P('kvh', 'ctx')
Inputs may be any that keep to these rules, and one draw needn't show every extreme that they name: `lengths`: some request has length 16 and some request has length 16384. slot_request is 12 for an empty slot; each page 0 to (lengths[r] - 1) // 256 of request r stands in exactly one slot, and no other page of it does. `slot_page`: 0 for an empty slot.
All inputs are finite; a program needn't handle non-finite values.
Results may differ from a plain program's by a relative error of at most 0.015.
Values may be sent and summed in bfloat16 or wider, within the bound.
No kernel may reach another device: no remote copies, remote signals or barrier semaphores. Data moves between devices by JAX's collectives and lax.ppermute only.
A program may use at most 128 MiB of HBM per device.

v0:
```python
import math

import jax
import jax.numpy as jnp
from jax import lax
from jax.sharding import PartitionSpec as P

QUERY_HEADS = 64
KEY_VALUE_HEADS = 8
DRAFT_TOKENS = 16


NEGATIVE_FLOOR = -1e30
PRECISE = lax.Precision.HIGHEST


def merged(part, axis, combine):
    gathered = jax.tree.map(lambda a: lax.all_gather(a, axis), part)

    def take(source):
        return jax.tree.map(lambda a: lax.dynamic_index_in_dim(a, source, 0, False), gathered)

    return lax.fori_loop(
        1, lax.axis_size(axis), lambda source, state: combine(state, take(source)), take(0)
    )


def fold_pages(running, block_data, query_lookup_table, lengths, draft, query_group_width):
    maxima, running_totals, output_rows = running
    key_block, value_block, page_request, page_index = block_data
    requests = query_lookup_table.shape[0]
    page_len = key_block.shape[2]
    head_dim = key_block.shape[3]
    request_ids = jnp.arange(requests, dtype=jnp.int32)
    belongs = page_request[:, None] == request_ids[None, :]
    onehot = belongs.astype(jnp.float32)
    chosen = jnp.einsum(
        "br,rhqd->bhqd",
        belongs.astype(jnp.bfloat16),
        query_lookup_table,
        preferred_element_type=jnp.float32,
    ).astype(jnp.bfloat16)
    scores = jnp.einsum(
        "bhqd,bhkd->bhqk", chosen, key_block, preferred_element_type=jnp.float32
    ) * (1.0 / math.sqrt(head_dim))
    own_length = jnp.sum(jnp.where(belongs, lengths[None, :], 0), axis=1)
    draft_row = jnp.arange(query_lookup_table.shape[2], dtype=jnp.int32) // query_group_width
    query_pos = own_length[:, None] - draft + draft_row[None, :]
    key_pos = page_index[:, None] * page_len + jnp.arange(page_len, dtype=jnp.int32)[None, :]
    visible = (page_request < requests)[:, None, None] & (
        key_pos[:, None, :] <= query_pos[:, :, None]
    )
    visible = visible[:, None, :, :]
    masked = jnp.where(visible, scores, NEGATIVE_FLOOR)
    page_max = jnp.max(masked, axis=3)
    weights = jnp.where(visible, jnp.exp(masked - page_max[..., None]), 0.0)
    page_mass = jnp.sum(weights, axis=3)
    page_out = jnp.einsum(
        "bhqk,bhkd->bhqd",
        weights.astype(jnp.bfloat16),
        value_block,
        preferred_element_type=jnp.float32,
    )
    request_max = jnp.max(
        jnp.where(belongs[:, :, None, None], page_max[:, None], NEGATIVE_FLOOR), axis=0
    )
    new_maxima = jnp.maximum(maxima, request_max)
    carry_keep = jnp.exp(maxima - new_maxima)
    page_ref = jnp.einsum("br,rhq->bhq", onehot, new_maxima, precision=PRECISE)
    factor = jnp.exp(page_max - page_ref)
    running_totals = running_totals * carry_keep + jnp.einsum(
        "br,bhq->rhq", onehot, page_mass * factor, precision=PRECISE
    )
    output_rows = output_rows * carry_keep[..., None] + jnp.einsum(
        "br,bhqd->rhqd", onehot, page_out * factor[..., None], precision=PRECISE
    )
    return (new_maxima, running_totals, output_rows)


def combine(earlier, later):
    max_one, sum_one, out_one = earlier
    max_two, sum_two, out_two = later
    joined = jnp.maximum(max_one, max_two)
    scale_one = jnp.exp(max_one - joined)
    scale_two = jnp.exp(max_two - joined)
    return (
        joined,
        sum_one * scale_one + sum_two * scale_two,
        out_one * scale_one[..., None] + out_two * scale_two[..., None],
    )


def per_device(queries, keys, values, out_weight, lengths, slot_request, slot_page):
    requests = queries.shape[0]
    kv_local = keys.shape[1]
    head_dim = keys.shape[3]
    query_group_width = QUERY_HEADS // KEY_VALUE_HEADS
    query_matrix_rows = DRAFT_TOKENS * query_group_width
    query_lookup_table = (
        queries.reshape(requests, DRAFT_TOKENS, kv_local, query_group_width, head_dim)
        .transpose(0, 2, 1, 3, 4)
        .reshape(requests, kv_local, query_matrix_rows, head_dim)
    )
    slot_total = keys.shape[0]
    pages_per_block = 4
    block_total = slot_total // pages_per_block

    def visit(counter, running):
        first_slot = counter * pages_per_block
        block_data = tuple(
            (
                lax.dynamic_slice_in_dim(source, first_slot, pages_per_block, 0)
                for source in (keys, values, slot_request, slot_page)
            )
        )
        return fold_pages(
            running, block_data, query_lookup_table, lengths, DRAFT_TOKENS, query_group_width
        )

    initial_state = (
        jnp.full((requests, kv_local, query_matrix_rows), NEGATIVE_FLOOR, jnp.float32),
        jnp.zeros((requests, kv_local, query_matrix_rows), jnp.float32),
        jnp.zeros((requests, kv_local, query_matrix_rows, head_dim), jnp.float32),
    )
    maxima, running_totals, output_rows = lax.fori_loop(0, block_total, visit, initial_state)
    maxima, running_totals, output_rows = merged(
        (maxima, running_totals, output_rows), "ctx", combine
    )
    attended_output = (output_rows / running_totals[..., None]).astype(jnp.bfloat16)
    attended_output = (
        attended_output.reshape(requests, kv_local, DRAFT_TOKENS, query_group_width, head_dim)
        .transpose(0, 2, 1, 3, 4)
        .reshape(requests * DRAFT_TOKENS, kv_local * query_group_width * head_dim)
    )
    return lax.psum_scatter(
        jnp.dot(attended_output, out_weight, preferred_element_type=jnp.float32).astype(
            jnp.bfloat16
        ),
        "kvh",
        scatter_dimension=0,
        tiled=True,
    )


def solution(mesh):
    placed = (
        P(None, None, "kvh"),
        P("ctx", "kvh", None, None),
        P("ctx", "kvh", None, None),
        P("kvh", "ctx"),
        P(),
        P("ctx"),
        P("ctx"),
    )
    return jax.shard_map(
        per_device, mesh=mesh, in_specs=placed, out_specs=P("kvh", "ctx"), check_vma=False
    )
```

profile of v0, /device:TPU:0, one launch (start us, length us, event | category | flops | bytes accessed | tf_op | source)
XLA Modules:
  0.0 380.0 jit_solution(2388794348547006236)
XLA Ops:
  9.7 139.4 %while.40 = (s32[]{:T(128)}, f32[12,2,128]{2,0,1:T(8,128)S(1)}, f32[12,2,128]{2,0,1:T(8,128)S(1)}, f32[12,2,128,128]{3,0,2,1:T(8,128)S(1)}, s32[64]{0:T(128)S(1)...) while((s32[]{:T(128)}, f32[12,2,128]{2,0,1:T(8,128)S(1)}, ...), condition=%wide.region_5.6_spmd.clone, body=%wide.region_0.5_spmd.clone.sunk | while | flops 160638864 | bytes 10442431 | solution.py:125
  16.1 2.2 fusion.60
  33.6 2.2 fusion.60
  42.3 2.2 fusion.60
  59.7 2.2 fusion.60
  77.1 2.2 fusion.60
  85.9 2.2 fusion.60
  103.3 2.2 fusion.60
  120.7 2.2 fusion.60
  129.4 2.2 fusion.60
  146.9 2.2 fusion.60
  150.9 33.0 %all-gather.1 = f32[96,2,128]{2,1,0:T(2,128)S(1)} all-gather(f32[12,2,128]{2,1,0:T(2,128)S(1)} %copy.52), channel_id=3, replica_groups=mesh['ctx'=8,'kvh'=4] {'ctx'}, dimensions={0}, use_global_device_ids=true | all-gather | bytes 110592 | tf_op jit(solution)/shard_map/all_gather | solution.py:18
  183.9 31.5 %all-gather = f32[96,2,128]{2,1,0:T(2,128)S(1)} all-gather(f32[12,2,128]{2,1,0:T(2,128)S(1)} %copy.51), channel_id=2, replica_groups=mesh['ctx'=8,'kvh'=4] {'ctx'}, dimensions={0}, use_global_device_ids=true | all-gather | bytes 110592 | tf_op jit(solution)/shard_map/all_gather | solution.py:18
  215.4 115.9 %all-gather.5.cloned.1.call-done = f32[96,2,128,128]{3,2,1,0:T(8,128)} async-done(((f32[12,2,128,128]{3,2,1,0:T(8,128)}), f32[96,2,128,128]{3,2,1,0:T(8,128)}) %all-gather.5.cloned.1.call-update) | async-done | bytes 12582928 | tf_op jit(solution)/shard_map/all_gather | solution.py:18
  332.8 16.3 %while.39 = (s32[]{:T(128)}, f32[12,2,128]{2,1,0:T(2,128)S(1)}, f32[12,2,128]{2,1,0:T(2,128)S(1)}, f32[12,2,128,128]{3,2,1,0:T(8,128)S(1)}, f32[8,12,2,128]{3,2,...) while((s32[]{:T(128)}, f32[12,2,128]{2,1,0:T(2,128)S(1)}, ...), condition=%wide.region_7.8_spmd, body=%wide.region_6.7_spmd.sunk | while | flops 1198085 | bytes 4841615 | solution.py:23
  332.9 2.3 fusion.47
  335.2 2.3 fusion.47
  337.6 2.3 fusion.47
  339.9 2.3 fusion.47
  342.2 2.3 fusion.47
  344.6 2.3 fusion.47
  346.9 2.3 fusion.47
  350.0 3.9 %convolution_convert_fusion.1 = bf16[192,1024]{1,0:T(8,128)(2,1)} fusion(bf16[192,2048]{1,0:T(8,128)(2,1)S(1)} %reshape.118, bf16[2048,1024]{1,0:T(8,128)(2,1)} %param.14), kind=kOutput, calls=%fused_computation.52 | convolution fusion | flops 805502976 | bytes 5373952 | tf_op jit(solution)/shard_map/dot_general | solution.py:136
  353.9 19.2 %reduce-scatter.2.cloned.1.call-done = bf16[48,1024]{1,0:T(8,128)(2,1)} async-done(((bf16[192,1024]{1,0:T(8,128)(2,1)}), bf16[48,1024]{1,0:T(8,128)(2,1)}) %reduce-scatter.2.cloned.1.call-update) | async-done | bytes 98320 | tf_op jit(solution)/shard_map/reduce_scatter | solution.py:135
  (372 shorter events, 123.0 us)
Async XLA Ops:
  6.5 3.1 copy-start.1
  6.5 3.1 copy-start
  6.5 3.1 copy-start.2
  6.5 324.8 %all-gather.5.cloned.1.call-start = ((), (), s32[]{:S(2)}) async-start(), calls=%async_computation.2 | async-start | bytes 14155776 | tf_op jit(solution)/shard_map/all_gather | solution.py:18
  150.8 222.3 %reduce-scatter.2.cloned.1.call-start = ((), (), s32[]{:S(2)}) async-start(), calls=%async_computation.1 | async-start | bytes 491520 | tf_op jit(solution)/shard_map/reduce_scatter | solution.py:135
Sparse Core Ops, SparseCore 0:
  150.9 180.3 all-gather.4
  354.1 19.0 reduce-scatter.1
where the time goes:
time: 383 us; the launch traced here: 380 us
  waiting for transfers between devices  135 us (35%)
  matrix products  118 us (31%)
  blocking collectives  64.5 us (17%)
  other arithmetic  36.8 us (10%)
  between operations  13.5 us (4%)
  local copies, waits for them, and re-layouts  10.5 us (3%)
    all_gather x1, waiting for transfers between devices, merged(): gathered = jax.tree.map(lambda a: lax.all_gather(a, axis), part)  116 us
    all_gather x2, blocking collectives, merged(): gathered = jax.tree.map(lambda a: lax.all_gather(a, axis), part)  64.5 us
    dot_general x16, matrix products, fold_pages(): jnp.einsum('br,bhqd->rhqd', onehot, page_out * factor[..., None], precisi...  35.9 us
    dot_general x16, matrix products, fold_pages(): jnp.einsum('br,rhqd->bhqd', belongs.astype(jnp.bfloat16), query_lookup_ta...  25.2 us
    dot_general x16, matrix products, fold_pages(): jnp.einsum('bhqd,bhkd->bhqk', chosen, key_block, preferred_element_type=j...  22.9 us
    dot_general x16, matrix products, fold_pages(): jnp.einsum('bhqk,bhkd->bhqd', weights.astype(jnp.bfloat16), value_block,...  22.9 us
    reduce_scatter x1, waiting for transfers between devices, per_device(): lax.psum_scatter(jnp.dot(attended_output, out_weight, preferred_element_t...  19.2 us
    add x7, other arithmetic, combine(): out_one * scale_one[..., None] + out_two * scale_two[..., None]  15.8 us
  transfers between devices with their start and end apart: 2, of which 2 were waited for; matrix products, arithmetic and copies ran while one was open for 0% of the time, Pallas kernels for 0%

commit v1 on v0

v1 whole, which is shorter than its diff:
```python
import functools
import math

import jax
import jax.numpy as jnp
from jax import lax
from jax.experimental import pallas as pl
from jax.experimental.pallas import tpu as pltpu
from jax.sharding import PartitionSpec as P

QUERY_HEADS = 64
KEY_VALUE_HEADS = 8
GROUP = QUERY_HEADS // KEY_VALUE_HEADS
DRAFT = 16
FLOOR = -1e30
LANES = 128
CHUNK = 4
UNROLL = 2


def attention_kernel(
    n_ctx, hps, tg,
    len_ref, req_ref, page_ref, q_ref, k_hbm, v_hbm, *rest,
):
    msgs = rest[:n_ctx]
    k_buf, v_buf, acc, top, mass, sems = rest[n_ctx:]
    slots, kv_local, page_len, head = k_hbm.shape
    requests = q_ref.shape[0]
    chunks = slots // CHUNK
    rows = GROUP * DRAFT
    scale = math.log2(math.e) / math.sqrt(head)

    def copies(i):
        at = pl.ds(i * CHUNK, CHUNK)
        return (
            pltpu.make_async_copy(k_hbm.at[at], k_buf.at[at], sems.at[0, i]),
            pltpu.make_async_copy(v_hbm.at[at], v_buf.at[at], sems.at[1, i]),
        )

    @pl.loop(0, chunks)
    def _(i):
        for copy in copies(i):
            copy.start()

    @pl.loop(0, requests)
    def _(r):
        top[r] = jnp.full(top.shape[1:], FLOOR, jnp.float32)
        mass[r] = jnp.zeros(mass.shape[1:], jnp.float32)
        acc[r] = jnp.zeros(acc.shape[1:], jnp.float32)

    ones = jnp.ones((page_len, LANES), jnp.bfloat16)
    offset = (
        lax.broadcasted_iota(jnp.int32, (rows, page_len), 1)
        - lax.broadcasted_iota(jnp.int32, (rows, page_len), 0) % DRAFT
    )

    def step(first, masked):
        work = []
        for u in range(UNROLL):
            s = first + u
            r = req_ref[s]
            r_in = jnp.minimum(r, requests - 1)
            last = len_ref[r_in] - DRAFT - page_ref[s] * page_len
            for h in range(kv_local):
                q = jnp.concatenate(
                    [q_ref[r_in, :, pl.ds((h * GROUP + g) * head, head)] for g in range(GROUP)], axis=0
                )
                scores = lax.dot_general(
                    q, k_buf[s, h], (((1,), (1,)), ((), ())), preferred_element_type=jnp.float32
                )
                if masked:
                    scores = jnp.where(offset <= last, scores, FLOOR)
                work.append((s, r, h, scores, jnp.max(scores, axis=1, keepdims=True)))
        weighted = []
        for s, r, h, scores, high in work:
            before = top[r, h]
            after = jnp.maximum(before, high)
            top[r, h] = after
            weights = jnp.concatenate(
                [
                    jnp.exp2((scores[:, i : i + LANES] - after) * scale).astype(jnp.bfloat16)
                    for i in range(0, page_len, LANES)
                ],
                axis=1,
            )
            weighted.append((s, r, h, weights, jnp.exp2((before - after) * scale)))
        for s, r, h, weights, keep in weighted:
            both = jnp.dot(
                weights,
                jnp.concatenate([v_buf[s, h], ones], axis=1),
                preferred_element_type=jnp.float32,
            )
            acc[r, h] = acc[r, h] * keep + both[:, :head]
            mass[r, h] = mass[r, h] * keep + both[:, head:]

    @pl.loop(0, chunks)
    def _(i):
        for copy in copies(i):
            copy.wait()

        @pl.loop(0, CHUNK // UNROLL)
        def _(j):
            first = i * CHUNK + j * UNROLL
            cut = False
            for u in range(UNROLL):
                s = first + u
                r = req_ref[s]
                r_in = jnp.minimum(r, requests - 1)
                end = page_ref[s] * page_len + page_len - 1
                cut = cut | ((r < requests) & (end > len_ref[r_in] - DRAFT))

            @pl.when(cut)
            def _():
                step(first, True)

            @pl.when(jnp.logical_not(cut))
            def _():
                step(first, False)

    me = lax.axis_index("ctx")
    per = requests // tg
    width = hps * LANES
    group = width // 4
    lane = lax.broadcasted_iota(jnp.int32, (DRAFT, LANES), 1)
    for d in range(n_ctx):
        dest = me ^ d
        part = dest % tg
        first_head = dest // tg * hps
        stat = [jnp.zeros((DRAFT, LANES), jnp.float32) for _ in range(hps)]

        def put(at, value):
            stat[at // LANES] = jnp.where(lane == at % LANES, value, stat[at // LANES])

        for rr in range(per):
            r = part * per + rr
            for hh in range(hps):
                q_head = first_head + hh
                h, g = q_head // GROUP, q_head % GROUP
                at = pl.ds(g * DRAFT, DRAFT)
                m = top[r, h, at, :]
                l = mass[r, h, at, :]
                o = acc[r, h, at, :]
                msgs[d][rr * DRAFT : (rr + 1) * DRAFT, hh * LANES : (hh + 1) * LANES] = (
                    o / jnp.where(l > 0, l, 1.0)
                ).astype(jnp.bfloat16)
                m_sent = m.astype(jnp.bfloat16).astype(jnp.float32)
                l_sent = jnp.where(m > 0.5 * FLOOR, l * jnp.exp2((m - m_sent) * scale), 0.0)
                l_high = l_sent.astype(jnp.bfloat16).astype(jnp.float32)
                t = rr * hps + hh
                put(t, m_sent)
                put(group + t, l_high)
                put(2 * group + t, l_sent - l_high)
        msgs[d][per * DRAFT :, :] = jnp.concatenate(stat, axis=1).astype(jnp.bfloat16)


def combine_kernel(n_ctx, scale, *refs):
    parts, out = refs[:n_ctx], refs[n_ctx]
    rows, width = out.shape
    per, hps, group = rows // DRAFT, width // LANES, width // 4
    tops, masses = [], []
    for p in parts:
        stat = p[rows:, :].astype(jnp.float32)
        tops.append(stat[:, :group])
        masses.append(stat[:, group : 2 * group] + stat[:, 2 * group : 3 * group])
    best = functools.reduce(jnp.maximum, tops)
    shares = [l * jnp.exp2((m - best) * scale) for m, l in zip(tops, masses)]
    total = functools.reduce(jnp.add, shares)
    lanes = lax.broadcasted_iota(jnp.int32, total.shape, 1)
    inverse = 1.0 / jnp.where(lanes < per * hps, total, 1.0)
    shares = [s * inverse for s in shares]
    for rr in range(per):
        for hh in range(hps):
            t = rr * hps + hh
            at = (slice(rr * DRAFT, (rr + 1) * DRAFT), slice(hh * LANES, (hh + 1) * LANES))
            out[at] = functools.reduce(
                jnp.add,
                [s[:, t : t + 1] * p[at].astype(jnp.float32) for s, p in zip(shares, parts)],
            ).astype(jnp.bfloat16)


def project_kernel(n_ctx, n_kvh, tg, *refs):
    parts, w_ref = refs[:n_ctx], refs[n_ctx]
    outs = refs[n_ctx + 1 : n_ctx + 1 + n_kvh]
    a_buf, total = refs[n_ctx + 1 + n_kvh :]
    rows, width = parts[0].shape
    me = lax.axis_index("ctx")
    for d, p in enumerate(parts):
        source = me ^ d
        a_buf[
            pl.ds(pl.multiple_of(source % tg * rows, rows), rows),
            pl.ds(pl.multiple_of(source // tg * width, width), width),
        ] = p[...]
    total[...] = jnp.dot(a_buf[...], w_ref[...], preferred_element_type=jnp.float32)
    mine = lax.axis_index("kvh")
    count = outs[0].shape[0]
    for d, o in enumerate(outs):
        o[...] = total[pl.ds(pl.multiple_of((mine ^ d) * count, 8), count), :].astype(jnp.bfloat16)


def exchange(x, axis, d):
    return lax.ppermute(x, axis, [(i, i ^ d) for i in range(lax.axis_size(axis))])


def per_device(queries, keys, values, out_weight, lengths, slot_request, slot_page):
    n_ctx, n_kvh = lax.axis_size("ctx"), lax.axis_size("kvh")
    requests = queries.shape[0]
    slots, kv_local, page_len, head = keys.shape
    heads = kv_local * GROUP
    hps, tg = max(heads // n_ctx, 1), max(n_ctx // heads, 1)
    tokens = requests * DRAFT
    rows, width = tokens // tg, hps * head
    unit = GROUP * DRAFT
    smem = pl.BlockSpec(memory_space=pltpu.SMEM)
    vmem = pl.BlockSpec(memory_space=pltpu.VMEM)
    hbm = pl.BlockSpec(memory_space=pl.ANY)
    params = pltpu.CompilerParams(vmem_limit_bytes=48 * 2**20)
    msgs = pl.pallas_call(
        functools.partial(attention_kernel, n_ctx, hps, tg),
        out_shape=[jax.ShapeDtypeStruct((rows + DRAFT, width), jnp.bfloat16)] * n_ctx,
        in_specs=[smem, smem, smem, vmem, hbm, hbm],
        out_specs=[vmem] * n_ctx,
        scratch_shapes=[
            pltpu.VMEM(keys.shape, keys.dtype),
            pltpu.VMEM(values.shape, values.dtype),
            pltpu.VMEM((requests + 1, kv_local, unit, head), jnp.float32),
            pltpu.VMEM((requests + 1, kv_local, unit, head), jnp.float32),
            pltpu.VMEM((requests + 1, kv_local, unit, head), jnp.float32),
            pltpu.SemaphoreType.DMA((2, slots // CHUNK)),
        ],
        compiler_params=params,
    )(lengths, slot_request, slot_page, queries, keys, values)
    got = [msgs[0]] + [exchange(msgs[d], "ctx", d) for d in range(1, n_ctx)]
    scale = math.log2(math.e) / math.sqrt(head)
    attended = pl.pallas_call(
        functools.partial(combine_kernel, n_ctx, scale),
        out_shape=jax.ShapeDtypeStruct((rows, width), jnp.bfloat16),
        in_specs=[vmem] * n_ctx,
        out_specs=vmem,
        compiler_params=params,
    )(*got)
    every = [attended] + [exchange(attended, "ctx", d) for d in range(1, n_ctx)]
    columns = out_weight.shape[1]
    partial = pl.pallas_call(
        functools.partial(project_kernel, n_ctx, n_kvh, tg),
        out_shape=[jax.ShapeDtypeStruct((tokens // n_kvh, columns), jnp.bfloat16)] * n_kvh,
        in_specs=[vmem] * (n_ctx + 1),
        out_specs=[vmem] * n_kvh,
        scratch_shapes=[
            pltpu.VMEM((tokens, heads * head), jnp.bfloat16),
            pltpu.VMEM((tokens, columns), jnp.float32),
        ],
        compiler_params=params,
    )(*every, out_weight)
    sums = partial[0].astype(jnp.float32)
    for d in range(1, n_kvh):
        sums = sums + exchange(partial[d], "kvh", d).astype(jnp.float32)
    return sums.astype(jnp.bfloat16)


def solution(mesh):
    placed = (
        P(None, None, "kvh"),
        P("ctx", "kvh", None, None),
        P("ctx", "kvh", None, None),
        P("kvh", "ctx"),
        P(),
        P("ctx"),
        P("ctx"),
    )
    return jax.shard_map(
        per_device, mesh=mesh, in_specs=placed, out_specs=P("kvh", "ctx"), check_vma=False
    )
```

time: 383 us -> 78 us (0.20)
  matrix products: 118 us -> 0 us
  waiting for transfers between devices: 135 us -> 20.5 us
  blocking collectives: 64.5 us -> 0 us
  other arithmetic: 36.8 us -> 0.69 us
  starting transfers between devices: 0.04 us -> 32.4 us
  Pallas kernels: 0 us -> 21 us
  between operations: 13.5 us -> 0.05 us
  local copies, waits for them, and re-layouts: 10.5 us -> 3.1 us
    dot_general x97 -> x0, matrix products: 118 us -> none  [the longest x16 35.9 us: fold_pages(): jnp.einsum('br,bhqd->rhqd', onehot, page_out * factor[..., None], precisi...]
    all_gather x1 -> x0, waiting for transfers between devices: 116 us -> none  [merged(): gathered = jax.tree.map(lambda a: lax.all_gather(a, axis), part)]
    all_gather x2 -> x0, blocking collectives: 64.5 us -> none  [merged(): gathered = jax.tree.map(lambda a: lax.all_gather(a, axis), part)]
    ppermute x0 -> x17, starting transfers between devices: none -> 32.4 us  [exchange(): lax.ppermute(x, axis, [(i, i ^ d) for i in range(lax.axis_size(axis))])]
    pallas_call x0 -> x3, Pallas kernels: none -> 21 us  [the longest x1 19.1 us: per_device(): pl.pallas_call(functools.partial(attention_kernel, n_ctx, hps, tg), out_s...]
    ppermute x0 -> x17, waiting for transfers between devices: none -> 20.5 us  [exchange(): lax.ppermute(x, axis, [(i, i ^ d) for i in range(lax.axis_size(axis))])]
    reduce_scatter x1 -> x0, waiting for transfers between devices: 19.2 us -> none  [per_device(): lax.psum_scatter(jnp.dot(attended_output, out_weight, preferred_element_t...]
    add x46 -> x0, other arithmetic: 18.5 us -> none  [the longest x7 15.8 us: combine(): out_one * scale_one[..., None] + out_two * scale_two[..., None]]
  transfers between devices with their start and end apart: 2 -> 17, of which waited for: 2 -> 7; matrix products, arithmetic and copies ran while one was open for 0% -> 0% of each run, Pallas kernels for 0% -> 0%
where the time goes in v1:
time: 78 us; the launch traced here: 77.8 us
  starting transfers between devices  32.4 us (42%)
  Pallas kernels  21 us (27%)
  waiting for transfers between devices  20.5 us (26%)
  local copies, waits for them, and re-layouts  3.1 us (4%)
    ppermute x17, starting transfers between devices, exchange(): lax.ppermute(x, axis, [(i, i ^ d) for i in range(lax.axis_size(axis))])  32.4 us
    ppermute x17, waiting for transfers between devices, exchange(): lax.ppermute(x, axis, [(i, i ^ d) for i in range(lax.axis_size(axis))])  20.5 us
    pallas_call x1, Pallas kernels, per_device(): pl.pallas_call(functools.partial(attention_kernel, n_ctx, hps, tg), out_s...  19.1 us
    unnamed x10, local copies, waits for them, and re-layouts  3.1 us
  transfers between devices with their start and end apart: 17, of which 7 were waited for; matrix products, arithmetic and copies ran while one was open for 0% of the time, Pallas kernels for 0%

profile of v1, /device:TPU:0, one launch (start us, length us, event | category | flops | bytes accessed | tf_op | source)
XLA Modules:
  0.0 77.8 jit_solution(14072777078167212631)
XLA Ops:
  0.0 1.1 %copy-done.1 = bf16[12,16,2048]{2,1,0:T(8,128)(2,1)S(1)} copy-done((bf16[12,16,2048]{2,1,0:T(8,128)(2,1)S(1)}, bf16[12,16,2048]{2,1,0:T(8,128)(2,1)}, u32[]{:S(2)}) %copy-start.1) | copy-done | bytes 786456
  1.1 0.7 copy-done.2
  1.8 0.7 copy-done.3
  3.1 19.1 %shard_map.73 = (bf16[208,256]{1,0:T(8,128)(2,1)S(1)}, bf16[208,256]{1,0:T(8,128)(2,1)S(1)}, bf16[208,256]{1,0:T(8,128)(2,1)S(1)}, bf16[208,256]{1,0:T(8,128)(2,...) custom-call(s32[12]{0:T(128)S(1)} %copy-done.2, ...), custom_call_target="tpu_custom_call" | custom-call | tf_op jit(solution)/shard_map/pallas_call | solution.py:217
  22.3 3.0 %collective-permute-start = (bf16[208,256]{1,0:T(8,128)(2,1)S(1)}, bf16[208,256]{1,0:T(8,128)(2,1)S(1)}, u32[]{:S(2)}, u32[]{:S(2)}) collective-permute-start(bf16[208,256]{1,0:T(8,128)(2,1)S(1)} %get-tuple-element.18), channel_id=1, source_target_pairs={{0,4},{4,0},{8,12},{12,8},{16,20},{20,16},{24,28},{28,24},{1,5},{5... | collective-permute-start | bytes 319496 | tf_op jit(solution)/shard_map/ppermute | solution.py:201
  25.3 1.6 %collective-permute-start.1 = (bf16[208,256]{1,0:T(8,128)(2,1)S(1)}, bf16[208,256]{1,0:T(8,128)(2,1)S(1)}, u32[]{:S(2)}, u32[]{:S(2)}) collective-permute-start(bf16[208,256]{1,0:T(8,128)(2,1)S(1)} %get-tuple-element.19), channel_id=1, source_target_pairs={{0,8},{4,12},{8,0},{12,4},{16,24},{20,28},{24,16},{28,20},{1,9},{5... | collective-permute-start | bytes 319496 | tf_op jit(solution)/shard_map/ppermute | solution.py:201
  26.9 3.0 %collective-permute-start.3 = (bf16[208,256]{1,0:T(8,128)(2,1)S(1)}, bf16[208,256]{1,0:T(8,128)(2,1)S(1)}, u32[]{:S(2)}, u32[]{:S(2)}) collective-permute-start(bf16[208,256]{1,0:T(8,128)(2,1)S(1)} %get-tuple-element.21), channel_id=1, source_target_pairs={{0,16},{4,20},{8,24},{12,28},{16,0},{20,4},{24,8},{28,12},{1,17},{... | collective-permute-start | bytes 319496 | tf_op jit(solution)/shard_map/ppermute | solution.py:201
  29.9 1.3 %collective-permute-start.4 = (bf16[208,256]{1,0:T(8,128)(2,1)S(1)}, bf16[208,256]{1,0:T(8,128)(2,1)S(1)}, u32[]{:S(2)}, u32[]{:S(2)}) collective-permute-start(bf16[208,256]{1,0:T(8,128)(2,1)S(1)} %get-tuple-element.22), channel_id=1, source_target_pairs={{0,20},{4,16},{8,28},{12,24},{16,4},{20,0},{24,12},{28,8},{1,21},{... | collective-permute-start | bytes 319496 | tf_op jit(solution)/shard_map/ppermute | solution.py:201
  31.1 3.6 %collective-permute-start.5 = (bf16[208,256]{1,0:T(8,128)(2,1)S(1)}, bf16[208,256]{1,0:T(8,128)(2,1)S(1)}, u32[]{:S(2)}, u32[]{:S(2)}) collective-permute-start(bf16[208,256]{1,0:T(8,128)(2,1)S(1)} %get-tuple-element.23), channel_id=1, source_target_pairs={{0,24},{4,28},{8,16},{12,20},{16,8},{20,12},{24,0},{28,4},{1,25},{... | collective-permute-start | bytes 319496 | tf_op jit(solution)/shard_map/ppermute | solution.py:201
  34.9 11.2 %collective-permute-done.4.refs_5_ = bf16[208,256]{1,0:T(8,128)(2,1)S(1)} collective-permute-done((bf16[208,256]{1,0:T(8,128)(2,1)S(1)}, bf16[208,256]{1,0:T(8,128)(2,1)S(1)}, u32[]{:S(2)}, u32[]{:S(2)}) %collective-permute-start.4) | collective-permute-done | bytes 106528 | tf_op jit(solution)/shard_map/ppermute | solution.py:201
  46.1 0.8 shard_map.74.refs_0_
  46.8 3.3 %collective-permute-start.13 = (bf16[192,256]{1,0:T(8,128)(2,1)S(1)}, bf16[192,256]{1,0:T(8,128)(2,1)S(1)}, u32[]{:S(2)}, u32[]{:S(2)}) collective-permute-start(bf16[192,256]{1,0:T(8,128)(2,1)S(1)} %shard_map.74.refs_0_), channel_id=1, source_target_pairs={{0,28},{4,24},{8,20},{12,16},{16,12},{20,8},{24,4},{28,0},{1,29},{... | collective-permute-start | bytes 294920 | tf_op jit(solution)/shard_map/ppermute | solution.py:201
  50.1 1.0 %collective-permute-start.12 = (bf16[192,256]{1,0:T(8,128)(2,1)S(1)}, bf16[192,256]{1,0:T(8,128)(2,1)S(1)}, u32[]{:S(2)}, u32[]{:S(2)}) collective-permute-start(bf16[192,256]{1,0:T(8,128)(2,1)S(1)} %shard_map.74.refs_0_), channel_id=1, source_target_pairs={{0,24},{4,28},{8,16},{12,20},{16,8},{20,12},{24,0},{28,4},{1,25},{... | collective-permute-start | bytes 294920 | tf_op jit(solution)/shard_map/ppermute | solution.py:201
  51.1 4.3 %collective-permute-start.11 = (bf16[192,256]{1,0:T(8,128)(2,1)S(1)}, bf16[192,256]{1,0:T(8,128)(2,1)S(1)}, u32[]{:S(2)}, u32[]{:S(2)}) collective-permute-start(bf16[192,256]{1,0:T(8,128)(2,1)S(1)} %shard_map.74.refs_0_), channel_id=1, source_target_pairs={{0,20},{4,16},{8,28},{12,24},{16,4},{20,0},{24,12},{28,8},{1,21},{... | collective-permute-start | bytes 294920 | tf_op jit(solution)/shard_map/ppermute | solution.py:201
  55.4 2.7 %collective-permute-start.9 = (bf16[192,256]{1,0:T(8,128)(2,1)S(1)}, bf16[192,256]{1,0:T(8,128)(2,1)S(1)}, u32[]{:S(2)}, u32[]{:S(2)}) collective-permute-start(bf16[192,256]{1,0:T(8,128)(2,1)S(1)} %shard_map.74.refs_0_), channel_id=1, source_target_pairs={{0,12},{4,8},{8,4},{12,0},{16,28},{20,24},{24,20},{28,16},{1,13},{... | collective-permute-start | bytes 294920 | tf_op jit(solution)/shard_map/ppermute | solution.py:201
  58.1 5.3 %collective-permute-start.8 = (bf16[192,256]{1,0:T(8,128)(2,1)S(1)}, bf16[192,256]{1,0:T(8,128)(2,1)S(1)}, u32[]{:S(2)}, u32[]{:S(2)}) collective-permute-start(bf16[192,256]{1,0:T(8,128)(2,1)S(1)} %shard_map.74.refs_0_), channel_id=1, source_target_pairs={{0,8},{4,12},{8,0},{12,4},{16,24},{20,28},{24,16},{28,20},{1,9},{5... | collective-permute-start | bytes 294920 | tf_op jit(solution)/shard_map/ppermute | solution.py:201
  63.4 1.3 %collective-permute-start.7 = (bf16[192,256]{1,0:T(8,128)(2,1)S(1)}, bf16[192,256]{1,0:T(8,128)(2,1)S(1)}, u32[]{:S(2)}, u32[]{:S(2)}) collective-permute-start(bf16[192,256]{1,0:T(8,128)(2,1)S(1)} %shard_map.74.refs_0_), channel_id=1, source_target_pairs={{0,4},{4,0},{8,12},{12,8},{16,20},{20,16},{24,28},{28,24},{1,5},{5... | collective-permute-start | bytes 294920 | tf_op jit(solution)/shard_map/ppermute | solution.py:201
  64.8 2.3 %collective-permute-done.11.refs_5_ = bf16[192,256]{1,0:T(8,128)(2,1)S(1)} collective-permute-done((bf16[192,256]{1,0:T(8,128)(2,1)S(1)}, bf16[192,256]{1,0:T(8,128)(2,1)S(1)}, u32[]{:S(2)}, u32[]{:S(2)}) %collective-permute-start.11) | collective-permute-done | bytes 98336 | tf_op jit(solution)/shard_map/ppermute | solution.py:201
  67.3 1.7 %collective-permute-done.8.refs_2_ = bf16[192,256]{1,0:T(8,128)(2,1)S(1)} collective-permute-done((bf16[192,256]{1,0:T(8,128)(2,1)S(1)}, bf16[192,256]{1,0:T(8,128)(2,1)S(1)}, u32[]{:S(2)}, u32[]{:S(2)}) %collective-permute-start.8) | collective-permute-done | bytes 98336 | tf_op jit(solution)/shard_map/ppermute | solution.py:201
  69.0 1.1 %shard_map.75 = (bf16[48,1024]{1,0:T(8,128)(2,1)S(1)}, bf16[48,1024]{1,0:T(8,128)(2,1)S(1)}, bf16[48,1024]{1,0:T(8,128)(2,1)S(1)}, bf16[48,1024]{1,0:T(8,128)(2,1)S(1)}) custom-call(bf16[192,256]{1,0:T(8,128)(2,1)S(1)} %shard_map.74.refs_0_, bf16[192,256]{1,0:T(8,128)(2,1)S(1)} %collective-permute-done.7.refs_1_, ...), custom_call_target="tpu_custom_call" | custom-call | tf_op jit(solution)/shard_map/pallas_call | solution.py:243
  70.2 1.6 %collective-permute-start.15 = (bf16[48,1024]{1,0:T(8,128)(2,1)S(1)}, bf16[48,1024]{1,0:T(8,128)(2,1)S(1)}, u32[]{:S(2)}, u32[]{:S(2)}) collective-permute-start(bf16[48,1024]{1,0:T(8,128)(2,1)S(1)} %get-tuple-element.27), channel_id=1, source_target_pairs={{0,2},{1,3},{2,0},{3,1},{4,6},{5,7},{6,4},{7,5},{8,10},{9,11},{10,... | collective-permute-start | bytes 294920 | tf_op jit(solution)/shard_map/ppermute | solution.py:201
  72.1 3.8 %collective-permute-done.15 = bf16[48,1024]{1,0:T(8,128)(2,1)S(1)} collective-permute-done((bf16[48,1024]{1,0:T(8,128)(2,1)S(1)}, bf16[48,1024]{1,0:T(8,128)(2,1)S(1)}, u32[]{:S(2)}, u32[]{:S(2)}) %collective-permute-start.15) | collective-permute-done | bytes 98336 | tf_op jit(solution)/shard_map/ppermute | solution.py:201
  75.9 1.2 %collective-permute-done.16 = bf16[48,1024]{1,0:T(8,128)(2,1)S(1)} collective-permute-done((bf16[48,1024]{1,0:T(8,128)(2,1)S(1)}, bf16[48,1024]{1,0:T(8,128)(2,1)S(1)}, u32[]{:S(2)}, u32[]{:S(2)}) %collective-permute-start.16) | collective-permute-done | bytes 98336 | tf_op jit(solution)/shard_map/ppermute | solution.py:201
  77.1 0.7 add_convert_fusion
  (24 shorter events, 1.4 us)
Async XLA Ops:
  0.0 1.1 %copy-start.1 = (bf16[12,16,2048]{2,1,0:T(8,128)(2,1)S(1)}, bf16[12,16,2048]{2,1,0:T(8,128)(2,1)}, u32[]{:S(2)}) copy-start(bf16[12,16,2048]{2,1,0:T(8,128)(2,1)} %q_ref.1) | copy-start | bytes 2359300
  1.1 0.7 copy-start.2
  1.8 0.7 copy-start.3
  2.4 0.7 copy-start.4
  3.1 65.9 %copy-start = (bf16[2048,1024]{1,0:T(8,128)(2,1)S(1)}, bf16[2048,1024]{1,0:T(8,128)(2,1)}, u32[]{:S(2)}) copy-start(bf16[2048,1024]{1,0:T(8,128)(2,1)} %refs_8_.1) | copy-start | bytes 12582916
  22.3 8.9 %collective-permute-start = (bf16[208,256]{1,0:T(8,128)(2,1)S(1)}, bf16[208,256]{1,0:T(8,128)(2,1)S(1)}, u32[]{:S(2)}, u32[]{:S(2)}) collective-permute-start(bf16[208,256]{1,0:T(8,128)(2,1)S(1)} %get-tuple-element.18), channel_id=1, source_target_pairs={{0,4},{4,0},{8,12},{12,8},{16,20},{20,16},{24,28},{28,24},{1,5},{5... | collective-permute-start | bytes 319496 | tf_op jit(solution)/shard_map/ppermute | solution.py:201
  25.3 9.5 %collective-permute-start.1 = (bf16[208,256]{1,0:T(8,128)(2,1)S(1)}, bf16[208,256]{1,0:T(8,128)(2,1)S(1)}, u32[]{:S(2)}, u32[]{:S(2)}) collective-permute-start(bf16[208,256]{1,0:T(8,128)(2,1)S(1)} %get-tuple-element.19), channel_id=1, source_target_pairs={{0,8},{4,12},{8,0},{12,4},{16,24},{20,28},{24,16},{28,20},{1,9},{5... | collective-permute-start | bytes 319496 | tf_op jit(solution)/shard_map/ppermute | solution.py:201
  26.9 7.9 %collective-permute-start.2 = (bf16[208,256]{1,0:T(8,128)(2,1)S(1)}, bf16[208,256]{1,0:T(8,128)(2,1)S(1)}, u32[]{:S(2)}, u32[]{:S(2)}) collective-permute-start(bf16[208,256]{1,0:T(8,128)(2,1)S(1)} %get-tuple-element.20), channel_id=1, source_target_pairs={{0,12},{4,8},{8,4},{12,0},{16,28},{20,24},{24,20},{28,16},{1,13},{... | collective-permute-start | bytes 319496 | tf_op jit(solution)/shard_map/ppermute | solution.py:201
  26.9 8.0 %collective-permute-start.3 = (bf16[208,256]{1,0:T(8,128)(2,1)S(1)}, bf16[208,256]{1,0:T(8,128)(2,1)S(1)}, u32[]{:S(2)}, u32[]{:S(2)}) collective-permute-start(bf16[208,256]{1,0:T(8,128)(2,1)S(1)} %get-tuple-element.21), channel_id=1, source_target_pairs={{0,16},{4,20},{8,24},{12,28},{16,0},{20,4},{24,8},{28,12},{1,17},{... | collective-permute-start | bytes 319496 | tf_op jit(solution)/shard_map/ppermute | solution.py:201
  29.9 16.2 %collective-permute-start.4 = (bf16[208,256]{1,0:T(8,128)(2,1)S(1)}, bf16[208,256]{1,0:T(8,128)(2,1)S(1)}, u32[]{:S(2)}, u32[]{:S(2)}) collective-permute-start(bf16[208,256]{1,0:T(8,128)(2,1)S(1)} %get-tuple-element.22), channel_id=1, source_target_pairs={{0,20},{4,16},{8,28},{12,24},{16,4},{20,0},{24,12},{28,8},{1,21},{... | collective-permute-start | bytes 319496 | tf_op jit(solution)/shard_map/ppermute | solution.py:201
  31.1 14.9 %collective-permute-start.5 = (bf16[208,256]{1,0:T(8,128)(2,1)S(1)}, bf16[208,256]{1,0:T(8,128)(2,1)S(1)}, u32[]{:S(2)}, u32[]{:S(2)}) collective-permute-start(bf16[208,256]{1,0:T(8,128)(2,1)S(1)} %get-tuple-element.23), channel_id=1, source_target_pairs={{0,24},{4,28},{8,16},{12,20},{16,8},{20,12},{24,0},{28,4},{1,25},{... | collective-permute-start | bytes 319496 | tf_op jit(solution)/shard_map/ppermute | solution.py:201
  34.7 11.3 %collective-permute-start.6 = (bf16[208,256]{1,0:T(8,128)(2,1)S(1)}, bf16[208,256]{1,0:T(8,128)(2,1)S(1)}, u32[]{:S(2)}, u32[]{:S(2)}) collective-permute-start(bf16[208,256]{1,0:T(8,128)(2,1)S(1)} %get-tuple-element.24), channel_id=1, source_target_pairs={{0,28},{4,24},{8,20},{12,16},{16,12},{20,8},{24,4},{28,0},{1,29},{... | collective-permute-start | bytes 319496 | tf_op jit(solution)/shard_map/ppermute | solution.py:201
  46.8 11.3 %collective-permute-start.13 = (bf16[192,256]{1,0:T(8,128)(2,1)S(1)}, bf16[192,256]{1,0:T(8,128)(2,1)S(1)}, u32[]{:S(2)}, u32[]{:S(2)}) collective-permute-start(bf16[192,256]{1,0:T(8,128)(2,1)S(1)} %shard_map.74.refs_0_), channel_id=1, source_target_pairs={{0,28},{4,24},{8,20},{12,16},{16,12},{20,8},{24,4},{28,0},{1,29},{... | collective-permute-start | bytes 294920 | tf_op jit(solution)/shard_map/ppermute | solution.py:201
  50.1 13.3 %collective-permute-start.12 = (bf16[192,256]{1,0:T(8,128)(2,1)S(1)}, bf16[192,256]{1,0:T(8,128)(2,1)S(1)}, u32[]{:S(2)}, u32[]{:S(2)}) collective-permute-start(bf16[192,256]{1,0:T(8,128)(2,1)S(1)} %shard_map.74.refs_0_), channel_id=1, source_target_pairs={{0,24},{4,28},{8,16},{12,20},{16,8},{20,12},{24,0},{28,4},{1,25},{... | collective-permute-start | bytes 294920 | tf_op jit(solution)/shard_map/ppermute | solution.py:201
  51.1 16.0 %collective-permute-start.11 = (bf16[192,256]{1,0:T(8,128)(2,1)S(1)}, bf16[192,256]{1,0:T(8,128)(2,1)S(1)}, u32[]{:S(2)}, u32[]{:S(2)}) collective-permute-start(bf16[192,256]{1,0:T(8,128)(2,1)S(1)} %shard_map.74.refs_0_), channel_id=1, source_target_pairs={{0,20},{4,16},{8,28},{12,24},{16,4},{20,0},{24,12},{28,8},{1,21},{... | collective-permute-start | bytes 294920 | tf_op jit(solution)/shard_map/ppermute | solution.py:201
  55.4 11.9 %collective-permute-start.10 = (bf16[192,256]{1,0:T(8,128)(2,1)S(1)}, bf16[192,256]{1,0:T(8,128)(2,1)S(1)}, u32[]{:S(2)}, u32[]{:S(2)}) collective-permute-start(bf16[192,256]{1,0:T(8,128)(2,1)S(1)} %shard_map.74.refs_0_), channel_id=1, source_target_pairs={{0,16},{4,20},{8,24},{12,28},{16,0},{20,4},{24,8},{28,12},{1,17},{... | collective-permute-start | bytes 294920 | tf_op jit(solution)/shard_map/ppermute | solution.py:201
  55.4 11.9 %collective-permute-start.9 = (bf16[192,256]{1,0:T(8,128)(2,1)S(1)}, bf16[192,256]{1,0:T(8,128)(2,1)S(1)}, u32[]{:S(2)}, u32[]{:S(2)}) collective-permute-start(bf16[192,256]{1,0:T(8,128)(2,1)S(1)} %shard_map.74.refs_0_), channel_id=1, source_target_pairs={{0,12},{4,8},{8,4},{12,0},{16,28},{20,24},{24,20},{28,16},{1,13},{... | collective-permute-start | bytes 294920 | tf_op jit(solution)/shard_map/ppermute | solution.py:201
  58.1 10.9 %collective-permute-start.8 = (bf16[192,256]{1,0:T(8,128)(2,1)S(1)}, bf16[192,256]{1,0:T(8,128)(2,1)S(1)}, u32[]{:S(2)}, u32[]{:S(2)}) collective-permute-start(bf16[192,256]{1,0:T(8,128)(2,1)S(1)} %shard_map.74.refs_0_), channel_id=1, source_target_pairs={{0,8},{4,12},{8,0},{12,4},{16,24},{20,28},{24,16},{28,20},{1,9},{5... | collective-permute-start | bytes 294920 | tf_op jit(solution)/shard_map/ppermute | solution.py:201
  63.4 5.6 %collective-permute-start.7 = (bf16[192,256]{1,0:T(8,128)(2,1)S(1)}, bf16[192,256]{1,0:T(8,128)(2,1)S(1)}, u32[]{:S(2)}, u32[]{:S(2)}) collective-permute-start(bf16[192,256]{1,0:T(8,128)(2,1)S(1)} %shard_map.74.refs_0_), channel_id=1, source_target_pairs={{0,4},{4,0},{8,12},{12,8},{16,20},{20,16},{24,28},{28,24},{1,5},{5... | collective-permute-start | bytes 294920 | tf_op jit(solution)/shard_map/ppermute | solution.py:201
  70.2 1.9 %collective-permute-start.14 = (bf16[48,1024]{1,0:T(8,128)(2,1)S(1)}, bf16[48,1024]{1,0:T(8,128)(2,1)S(1)}, u32[]{:S(2)}, u32[]{:S(2)}) collective-permute-start(bf16[48,1024]{1,0:T(8,128)(2,1)S(1)} %get-tuple-element.26), channel_id=1, source_target_pairs={{0,1},{1,0},{2,3},{3,2},{4,5},{5,4},{6,7},{7,6},{8,9},{9,8},{10,11... | collective-permute-start | bytes 294920 | tf_op jit(solution)/shard_map/ppermute | solution.py:201
  70.2 5.7 %collective-permute-start.15 = (bf16[48,1024]{1,0:T(8,128)(2,1)S(1)}, bf16[48,1024]{1,0:T(8,128)(2,1)S(1)}, u32[]{:S(2)}, u32[]{:S(2)}) collective-permute-start(bf16[48,1024]{1,0:T(8,128)(2,1)S(1)} %get-tuple-element.27), channel_id=1, source_target_pairs={{0,2},{1,3},{2,0},{3,1},{4,6},{5,7},{6,4},{7,5},{8,10},{9,11},{10,... | collective-permute-start | bytes 294920 | tf_op jit(solution)/shard_map/ppermute | solution.py:201
  71.8 5.3 %collective-permute-start.16 = (bf16[48,1024]{1,0:T(8,128)(2,1)S(1)}, bf16[48,1024]{1,0:T(8,128)(2,1)S(1)}, u32[]{:S(2)}, u32[]{:S(2)}) collective-permute-start(bf16[48,1024]{1,0:T(8,128)(2,1)S(1)} %get-tuple-element.28), channel_id=1, source_target_pairs={{0,3},{1,2},{2,1},{3,0},{4,7},{5,6},{6,5},{7,4},{8,11},{9,10},{10,... | collective-permute-start | bytes 294920 | tf_op jit(solution)/shard_map/ppermute | solution.py:201

commit v2 on v1

v2 whole, which is shorter than its diff:
```python
import functools
import math

import jax
import jax.numpy as jnp
from jax import lax
from jax.experimental import pallas as pl
from jax.experimental.pallas import tpu as pltpu
from jax.sharding import PartitionSpec as P

QUERY_HEADS = 64
KEY_VALUE_HEADS = 8
GROUP = QUERY_HEADS // KEY_VALUE_HEADS
DRAFT = 16
FLOOR = -1e30
LANES = 128
CHUNK = 16
COPIES = 4


def attention_kernel(
    n_ctx, hps, tg,
    len_hbm, req_hbm, page_hbm, q_hbm, k_hbm, v_hbm, *rest,
):
    msgs = rest[:n_ctx]
    len_ref, req_ref, page_ref, q_ref, k_buf, v_buf, raw, top, acc, sems, head_sems = rest[n_ctx:]
    slots, kv_local, page_len, head = k_hbm.shape
    requests = q_ref.shape[0]
    chunks = slots // CHUNK
    rows = GROUP * DRAFT
    scale = math.log2(math.e) / math.sqrt(head)

    def load(i, which):
        size = CHUNK // COPIES
        at = pl.ds(i * size, size)
        source, target = ((k_hbm, k_buf), (v_hbm, v_buf))[which]
        return pltpu.make_async_copy(source.at[at], target.at[at], sems.at[which, i])

    def start(i, which):
        for c in range(COPIES):
            load(i * COPIES + c, which).start()

    def wait(i, which):
        for c in range(COPIES):
            load(i * COPIES + c, which).wait()

    first_loads = [
        pltpu.make_async_copy(source, target, head_sems.at[n])
        for n, (source, target) in enumerate(
            ((len_hbm, len_ref), (req_hbm, req_ref), (page_hbm, page_ref), (q_hbm, q_ref))
        )
    ]
    for copy in first_loads:
        copy.start()

    @pl.loop(0, chunks)
    def _(i):
        start(i, 0)

    @pl.loop(0, requests + 1)
    def _(r):
        top[r] = jnp.full(top.shape[1:], FLOOR, jnp.float32)
        acc[r] = jnp.zeros(acc.shape[1:], jnp.float32)

    for copy in first_loads:
        copy.wait()

    ones = jnp.ones((page_len, LANES), jnp.bfloat16)

    def score(first, masked):
        for u in range(CHUNK):
            s = first + u
            r = req_ref[s]
            r_in = jnp.minimum(r, requests - 1)
            for h in range(kv_local):
                q = jnp.concatenate(
                    [q_ref[r_in, :, pl.ds((h * GROUP + g) * head, head)] for g in range(GROUP)], axis=0
                )
                scores = lax.dot_general(
                    q, k_buf[s, h], (((1,), (1,)), ((), ())), preferred_element_type=jnp.float32
                )
                if masked:
                    last = len_ref[r_in] - DRAFT - page_ref[s] * page_len
                    offset = (
                        lax.broadcasted_iota(jnp.int32, (rows, page_len), 1)
                        - lax.broadcasted_iota(jnp.int32, (rows, page_len), 0) % DRAFT
                    )
                    scores = jnp.where(offset <= last, scores, FLOOR)
                raw[s, h] = scores
                high = functools.reduce(
                    jnp.maximum, [scores[:, i : i + LANES] for i in range(0, page_len, LANES)]
                )
                top[r, h] = jnp.maximum(top[r, h], high)

    @pl.loop(0, chunks)
    def _(i):
        start(i, 1)
        wait(i, 0)
        cut = False
        for u in range(CHUNK):
            s = i * CHUNK + u
            r = req_ref[s]
            end = page_ref[s] * page_len + page_len - 1
            cut = cut | ((r < requests) & (end > len_ref[jnp.minimum(r, requests - 1)] - DRAFT))

        @pl.when(cut)
        def _():
            score(i * CHUNK, True)

        @pl.when(jnp.logical_not(cut))
        def _():
            score(i * CHUNK, False)

    @pl.loop(0, requests)
    def _(r):
        for h in range(kv_local):
            top[r, h] = jnp.broadcast_to(
                jnp.max(top[r, h], axis=1, keepdims=True), (rows, LANES)
            )

    @pl.loop(0, chunks)
    def _(i):
        wait(i, 1)
        for u in range(CHUNK):
            s = i * CHUNK + u
            r = req_ref[s]
            for h in range(kv_local):
                high = top[r, h]
                weights = jnp.concatenate(
                    [
                        jnp.exp2((raw[s, h, :, i : i + LANES] - high) * scale).astype(jnp.bfloat16)
                        for i in range(0, page_len, LANES)
                    ],
                    axis=1,
                )
                acc[r, h] += jnp.dot(
                    weights,
                    jnp.concatenate([v_buf[s, h], ones], axis=1),
                    preferred_element_type=jnp.float32,
                )

    me = lax.axis_index("ctx")
    per = requests // tg
    width = hps * LANES
    group = width // 4
    lane = lax.broadcasted_iota(jnp.int32, (DRAFT, LANES), 1)
    for d in range(n_ctx):
        dest = me ^ d
        part = dest % tg
        first_head = dest // tg * hps
        tops = jnp.full((DRAFT, LANES), FLOOR, jnp.float32)
        sums = jnp.zeros((DRAFT, LANES), jnp.float32)
        for rr in range(per):
            r = part * per + rr
            for hh in range(hps):
                q_head = first_head + hh
                h, g = q_head // GROUP, q_head % GROUP
                at = pl.ds(g * DRAFT, DRAFT)
                m = top[r, h, at, :]
                l = acc[r, h, at, head:]
                o = acc[r, h, at, :head]
                msgs[d][rr * DRAFT : (rr + 1) * DRAFT, hh * LANES : (hh + 1) * LANES] = (
                    o * pl.reciprocal(jnp.where(l > 0, l, 1.0), approx=True)
                ).astype(jnp.bfloat16)
                t = rr * hps + hh
                tops = jnp.where(lane == t, m, tops)
                sums = jnp.where(lane == t, l, sums)
        tops_sent = tops.astype(jnp.bfloat16).astype(jnp.float32)
        sums = jnp.where(tops > 0.5 * FLOOR, sums * jnp.exp2((tops - tops_sent) * scale), 0.0)
        sums_high = sums.astype(jnp.bfloat16).astype(jnp.float32)
        msgs[d][per * DRAFT :, :] = jnp.concatenate(
            [x[:, :group] for x in (tops_sent, sums_high, sums - sums_high, sums)], axis=1
        ).astype(jnp.bfloat16)


def combine_kernel(final, scale, *refs):
    parts, out = refs[:-1], refs[-1]
    width = out.shape[1]
    rows = parts[0].shape[0] - DRAFT
    per, hps, group = rows // DRAFT, width // LANES, width // 4
    tops, masses = [], []
    for p in parts:
        stat = p[rows:, :].astype(jnp.float32)
        tops.append(stat[:, :group])
        masses.append(stat[:, group : 2 * group] + stat[:, 2 * group : 3 * group])
    best = functools.reduce(jnp.maximum, tops)
    shares = [l * jnp.exp2((m - best) * scale) for m, l in zip(tops, masses)]
    total = functools.reduce(jnp.add, shares)
    inverse = 1.0 / jnp.where(total > 0, total, 1.0)
    shares = [s * inverse for s in shares]
    for rr in range(per):
        for hh in range(hps):
            t = rr * hps + hh
            at = (slice(rr * DRAFT, (rr + 1) * DRAFT), slice(hh * LANES, (hh + 1) * LANES))
            out[at] = functools.reduce(
                jnp.add,
                [s[:, t : t + 1] * p[at].astype(jnp.float32) for s, p in zip(shares, parts)],
            ).astype(jnp.bfloat16)
    if not final:
        high = total.astype(jnp.bfloat16).astype(jnp.float32)
        out[rows:, :] = jnp.concatenate([best, high, total - high, total], axis=1).astype(jnp.bfloat16)


def project_kernel(n_ctx, n_kvh, tg, *refs):
    parts, w_ref = refs[:n_ctx], refs[n_ctx]
    outs = refs[n_ctx + 1 : n_ctx + 1 + n_kvh]
    a_buf, total = refs[n_ctx + 1 + n_kvh :]
    rows, width = parts[0].shape
    me = lax.axis_index("ctx")
    for d, p in enumerate(parts):
        source = me ^ d
        a_buf[
            pl.ds(pl.multiple_of(source % tg * rows, rows), rows),
            pl.ds(pl.multiple_of(source // tg * width, width), width),
        ] = p[...]
    total[...] = jnp.dot(a_buf[...], w_ref[...], preferred_element_type=jnp.float32)
    mine = lax.axis_index("kvh")
    count = outs[0].shape[0]
    for d, o in enumerate(outs):
        o[...] = total[pl.ds(pl.multiple_of((mine ^ d) * count, 8), count), :].astype(jnp.bfloat16)


def exchange(x, axis, d):
    return lax.ppermute(x, axis, [(i, i ^ d) for i in range(lax.axis_size(axis))])


def per_device(queries, keys, values, out_weight, lengths, slot_request, slot_page):
    n_ctx, n_kvh = lax.axis_size("ctx"), lax.axis_size("kvh")
    requests = queries.shape[0]
    slots, kv_local, page_len, head = keys.shape
    heads = kv_local * GROUP
    hps, tg = max(heads // n_ctx, 1), max(n_ctx // heads, 1)
    tokens = requests * DRAFT
    rows, width = tokens // tg, hps * head
    unit = GROUP * DRAFT
    smem = pl.BlockSpec(memory_space=pltpu.SMEM)
    vmem = pl.BlockSpec(memory_space=pltpu.VMEM)
    hbm = pl.BlockSpec(memory_space=pltpu.HBM)
    params = pltpu.CompilerParams(vmem_limit_bytes=46 * 2**20)
    small = pltpu.CompilerParams(vmem_limit_bytes=16 * 2**20)
    msgs = pl.pallas_call(
        functools.partial(attention_kernel, n_ctx, hps, tg),
        out_shape=[jax.ShapeDtypeStruct((rows + DRAFT, width), jnp.bfloat16)] * n_ctx,
        in_specs=[hbm] * 6,
        out_specs=[vmem] * n_ctx,
        scratch_shapes=[
            pltpu.SMEM(lengths.shape, jnp.int32),
            pltpu.SMEM(slot_request.shape, jnp.int32),
            pltpu.SMEM(slot_page.shape, jnp.int32),
            pltpu.VMEM(queries.shape, queries.dtype),
            pltpu.VMEM(keys.shape, keys.dtype),
            pltpu.VMEM(values.shape, values.dtype),
            pltpu.VMEM((slots, kv_local, unit, page_len), jnp.float32),
            pltpu.VMEM((requests + 1, kv_local, unit, LANES), jnp.float32),
            pltpu.VMEM((requests + 1, kv_local, unit, head + LANES), jnp.float32),
            pltpu.SemaphoreType.DMA((2, slots // CHUNK * COPIES)),
            pltpu.SemaphoreType.DMA((4,)),
        ],
        compiler_params=params,
    )(*(pltpu.with_memory_space_constraint(x, pltpu.HBM) for x in (lengths, slot_request, slot_page, queries)), keys, values)
    scale = math.log2(math.e) / math.sqrt(head)

    def combine(parts, final):
        shape = (rows if final else rows + DRAFT, width)
        return pl.pallas_call(
            functools.partial(combine_kernel, final, scale),
            out_shape=jax.ShapeDtypeStruct(shape, jnp.bfloat16),
            in_specs=[vmem] * len(parts),
            out_specs=vmem,
            compiler_params=small,
        )(*parts)

    across = sorted(range(0, n_ctx, 2), key=lambda d: (d == 0, d < 4, d))
    beside = {d: exchange(msgs[d + 1], "ctx", 1) for d in across}
    got = [exchange(combine([msgs[d], beside[d]], False), "ctx", d) for d in across[:-1]]
    attended = combine([msgs[0], beside[0], *got], True)
    every = {0: attended}
    for d in sorted(range(2, n_ctx, 2), key=lambda d: (d < 4, d)):
        every[d] = exchange(attended, "ctx", d)
    for d in sorted(range(0, n_ctx, 2), key=lambda d: (d != 0, d < 4, d)):
        every[d + 1] = exchange(every[d], "ctx", 1)
    every = [every[d] for d in range(n_ctx)]
    columns = out_weight.shape[1]
    partial = pl.pallas_call(
        functools.partial(project_kernel, n_ctx, n_kvh, tg),
        out_shape=[jax.ShapeDtypeStruct((tokens // n_kvh, columns), jnp.bfloat16)] * n_kvh,
        in_specs=[vmem] * (n_ctx + 1),
        out_specs=[vmem] * n_kvh,
        scratch_shapes=[
            pltpu.VMEM((tokens, heads * head), jnp.bfloat16),
            pltpu.VMEM((tokens, columns), jnp.float32),
        ],
        compiler_params=small,
    )(*every, out_weight)
    sums = partial[0].astype(jnp.float32)
    for d in range(1, n_kvh):
        sums = sums + exchange(partial[d], "kvh", d).astype(jnp.float32)
    return sums.astype(jnp.bfloat16)


def solution(mesh):
    placed = (
        P(None, None, "kvh"),
        P("ctx", "kvh", None, None),
        P("ctx", "kvh", None, None),
        P("kvh", "ctx"),
        P(),
        P("ctx"),
        P("ctx"),
    )
    return jax.shard_map(
        per_device, mesh=mesh, in_specs=placed, out_specs=P("kvh", "ctx"), check_vma=False
    )
```

time: 78 us -> 55.9 us (0.72)
  starting transfers between devices: 32.4 us -> 22.9 us
  Pallas kernels: 21 us -> 13.5 us
  local copies, waits for them, and re-layouts: 3.1 us -> 0.01 us
  waiting for transfers between devices: 20.5 us -> 18.7 us
    ppermute x17, starting transfers between devices: 32.4 us -> 22.9 us  [exchange(): lax.ppermute(x, axis, [(i, i ^ d) for i in range(lax.axis_size(axis))])]
    pallas_call x1, Pallas kernels: 19.1 us -> 11 us  [per_device(): pl.pallas_call(functools.partial(attention_kernel, n_ctx, hps, tg), out_s...]
    unnamed x10 -> x2, local copies, waits for them, and re-layouts: 3.1 us -> 0.01 us
    ppermute x17, waiting for transfers between devices: 20.5 us -> 18.7 us  [exchange(): lax.ppermute(x, axis, [(i, i ^ d) for i in range(lax.axis_size(axis))])]
  transfers between devices with their start and end apart: 17 -> 17, of which waited for: 7 -> 10; matrix products, arithmetic and copies ran while one was open for 0% -> 0% of each run, Pallas kernels for 0% -> 2%
where the time goes in v2:
time: 55.9 us; the launch traced here: 55.8 us
  starting transfers between devices  22.9 us (41%)
  waiting for transfers between devices  18.7 us (33%)
  Pallas kernels  13.5 us (24%)
  other arithmetic  0.69 us (1%)
    ppermute x17, starting transfers between devices, exchange(): lax.ppermute(x, axis, [(i, i ^ d) for i in range(lax.axis_size(axis))])  22.9 us
    ppermute x17, waiting for transfers between devices, exchange(): lax.ppermute(x, axis, [(i, i ^ d) for i in range(lax.axis_size(axis))])  18.7 us
    pallas_call x1, Pallas kernels, per_device(): pl.pallas_call(functools.partial(attention_kernel, n_ctx, hps, tg), out_s...  11 us
    pallas_call x4, Pallas kernels, combine(): pl.pallas_call(functools.partial(combine_kernel, final, scale), out_shape...  1.35 us
  transfers between devices with their start and end apart: 17, of which 10 were waited for; matrix products, arithmetic and copies ran while one was open for 0% of the time, Pallas kernels for 2%

profile of v2, /device:TPU:0, one launch (start us, length us, event | category | flops | bytes accessed | tf_op | source)
XLA Modules:
  0.0 55.8 jit_solution(5576039474518772034)
XLA Ops:
  0.0 11.0 %shard_map.73 = (bf16[208,256]{1,0:T(8,128)(2,1)S(1)}, bf16[208,256]{1,0:T(8,128)(2,1)S(1)}, bf16[208,256]{1,0:T(8,128)(2,1)S(1)}, bf16[208,256]{1,0:T(8,128)(2,...) custom-call(s32[12]{0:T(128)} %len_hbm.1, ...), custom_call_target="tpu_custom_call" | custom-call | tf_op jit(solution)/shard_map/pallas_call | solution.py:241
  11.0 3.0 %collective-permute-start.1 = (bf16[208,256]{1,0:T(8,128)(2,1)S(1)}, bf16[208,256]{1,0:T(8,128)(2,1)S(1)}, u32[]{:S(2)}, u32[]{:S(2)}) collective-permute-start(bf16[208,256]{1,0:T(8,128)(2,1)S(1)} %get-tuple-element.20), channel_id=1, source_target_pairs={{0,4},{4,0},{8,12},{12,8},{16,20},{20,16},{24,28},{28,24},{1,5},{5... | collective-permute-start | bytes 319496 | tf_op jit(solution)/shard_map/ppermute | solution.py:224
  14.1 1.9 %collective-permute-start.5 = (bf16[208,256]{1,0:T(8,128)(2,1)S(1)}, bf16[208,256]{1,0:T(8,128)(2,1)S(1)}, u32[]{:S(2)}, u32[]{:S(2)}) collective-permute-start(bf16[208,256]{1,0:T(8,128)(2,1)S(1)} %get-tuple-element.24), channel_id=1, source_target_pairs={{0,4},{4,0},{8,12},{12,8},{16,20},{20,16},{24,28},{28,24},{1,5},{5... | collective-permute-start | bytes 319496 | tf_op jit(solution)/shard_map/ppermute | solution.py:224
  16.1 1.7 %collective-permute-done.1.refs_1_ = bf16[208,256]{1,0:T(8,128)(2,1)S(1)} collective-permute-done((bf16[208,256]{1,0:T(8,128)(2,1)S(1)}, bf16[208,256]{1,0:T(8,128)(2,1)S(1)}, u32[]{:S(2)}, u32[]{:S(2)}) %collective-permute-start.1) | collective-permute-done | bytes 106528 | tf_op jit(solution)/shard_map/ppermute | solution.py:224
  18.1 3.3 %collective-permute-start.2 = (bf16[208,256]{1,0:T(8,128)(2,1)S(1)}, bf16[208,256]{1,0:T(8,128)(2,1)S(1)}, u32[]{:S(2)}, u32[]{:S(2)}) collective-permute-start(bf16[208,256]{1,0:T(8,128)(2,1)S(1)} %shard_map.74), channel_id=1, source_target_pairs={{0,16},{4,20},{8,24},{12,28},{16,0},{20,4},{24,8},{28,12},{1,17},{... | collective-permute-start | bytes 319496 | tf_op jit(solution)/shard_map/ppermute | solution.py:224
  21.7 2.8 %collective-permute-start.4 = (bf16[208,256]{1,0:T(8,128)(2,1)S(1)}, bf16[208,256]{1,0:T(8,128)(2,1)S(1)}, u32[]{:S(2)}, u32[]{:S(2)}) collective-permute-start(bf16[208,256]{1,0:T(8,128)(2,1)S(1)} %shard_map.75), channel_id=1, source_target_pairs={{0,24},{4,28},{8,16},{12,20},{16,8},{20,12},{24,0},{28,4},{1,25},{... | collective-permute-start | bytes 319496 | tf_op jit(solution)/shard_map/ppermute | solution.py:224
  24.9 2.3 %collective-permute-done.2.refs_2_ = bf16[208,256]{1,0:T(8,128)(2,1)S(1)} collective-permute-done((bf16[208,256]{1,0:T(8,128)(2,1)S(1)}, bf16[208,256]{1,0:T(8,128)(2,1)S(1)}, u32[]{:S(2)}, u32[]{:S(2)}) %collective-permute-start.2) | collective-permute-done | bytes 106528 | tf_op jit(solution)/shard_map/ppermute | solution.py:224
  27.2 1.2 %collective-permute-done.4.refs_3_ = bf16[208,256]{1,0:T(8,128)(2,1)S(1)} collective-permute-done((bf16[208,256]{1,0:T(8,128)(2,1)S(1)}, bf16[208,256]{1,0:T(8,128)(2,1)S(1)}, u32[]{:S(2)}, u32[]{:S(2)}) %collective-permute-start.4) | collective-permute-done | bytes 106528 | tf_op jit(solution)/shard_map/ppermute | solution.py:224
  28.4 1.2 %collective-permute-done.6.refs_4_ = bf16[208,256]{1,0:T(8,128)(2,1)S(1)} collective-permute-done((bf16[208,256]{1,0:T(8,128)(2,1)S(1)}, bf16[208,256]{1,0:T(8,128)(2,1)S(1)}, u32[]{:S(2)}, u32[]{:S(2)}) %collective-permute-start.6) | collective-permute-done | bytes 106528 | tf_op jit(solution)/shard_map/ppermute | solution.py:224
  30.1 3.3 %collective-permute-start.12 = (bf16[192,256]{1,0:T(8,128)(2,1)S(1)}, bf16[192,256]{1,0:T(8,128)(2,1)S(1)}, u32[]{:S(2)}, u32[]{:S(2)}) collective-permute-start(bf16[192,256]{1,0:T(8,128)(2,1)S(1)} %shard_map.77.refs_0_), channel_id=1, source_target_pairs={{0,24},{4,28},{8,16},{12,20},{16,8},{20,12},{24,0},{28,4},{1,25},{... | collective-permute-start | bytes 294920 | tf_op jit(solution)/shard_map/ppermute | solution.py:224
  33.4 1.1 %collective-permute-start.8 = (bf16[192,256]{1,0:T(8,128)(2,1)S(1)}, bf16[192,256]{1,0:T(8,128)(2,1)S(1)}, u32[]{:S(2)}, u32[]{:S(2)}) collective-permute-start(bf16[192,256]{1,0:T(8,128)(2,1)S(1)} %shard_map.77.refs_0_), channel_id=1, source_target_pairs={{0,8},{4,12},{8,0},{12,4},{16,24},{20,28},{24,16},{28,20},{1,9},{5... | collective-permute-start | bytes 294920 | tf_op jit(solution)/shard_map/ppermute | solution.py:224
  34.5 1.6 %collective-permute-start.7 = (bf16[192,256]{1,0:T(8,128)(2,1)S(1)}, bf16[192,256]{1,0:T(8,128)(2,1)S(1)}, u32[]{:S(2)}, u32[]{:S(2)}) collective-permute-start(bf16[192,256]{1,0:T(8,128)(2,1)S(1)} %shard_map.77.refs_0_), channel_id=1, source_target_pairs={{0,4},{4,0},{8,12},{12,8},{16,20},{20,16},{24,28},{28,24},{1,5},{5... | collective-permute-start | bytes 294920 | tf_op jit(solution)/shard_map/ppermute | solution.py:224
  36.2 0.6 %collective-permute-done.12.refs_6_ = bf16[192,256]{1,0:T(8,128)(2,1)S(1)} collective-permute-done((bf16[192,256]{1,0:T(8,128)(2,1)S(1)}, bf16[192,256]{1,0:T(8,128)(2,1)S(1)}, u32[]{:S(2)}, u32[]{:S(2)}) %collective-permute-start.12) | collective-permute-done | bytes 98336 | tf_op jit(solution)/shard_map/ppermute | solution.py:224
  36.8 1.5 %collective-permute-start.13 = (bf16[192,256]{1,0:T(8,128)(2,1)S(1)}, bf16[192,256]{1,0:T(8,128)(2,1)S(1)}, u32[]{:S(2)}, u32[]{:S(2)}) collective-permute-start(bf16[192,256]{1,0:T(8,128)(2,1)S(1)} %collective-permute-done.12.refs_6_), channel_id=1, source_target_pairs={{0,4},{4,0},{8,12},{12,8},{16,20},{20,16},{24,28},{28,24},{1,5},{5... | collective-permute-start | bytes 294920 | tf_op jit(solution)/shard_map/ppermute | solution.py:224
  38.3 2.6 %collective-permute-done.10.refs_4_ = bf16[192,256]{1,0:T(8,128)(2,1)S(1)} collective-permute-done((bf16[192,256]{1,0:T(8,128)(2,1)S(1)}, bf16[192,256]{1,0:T(8,128)(2,1)S(1)}, u32[]{:S(2)}, u32[]{:S(2)}) %collective-permute-start.10) | collective-permute-done | bytes 98336 | tf_op jit(solution)/shard_map/ppermute | solution.py:224
  40.9 1.4 %collective-permute-start.11 = (bf16[192,256]{1,0:T(8,128)(2,1)S(1)}, bf16[192,256]{1,0:T(8,128)(2,1)S(1)}, u32[]{:S(2)}, u32[]{:S(2)}) collective-permute-start(bf16[192,256]{1,0:T(8,128)(2,1)S(1)} %collective-permute-done.10.refs_4_), channel_id=1, source_target_pairs={{0,4},{4,0},{8,12},{12,8},{16,20},{20,16},{24,28},{28,24},{1,5},{5... | collective-permute-start | bytes 294920 | tf_op jit(solution)/shard_map/ppermute | solution.py:224
  42.3 0.6 %collective-permute-start.9 = (bf16[192,256]{1,0:T(8,128)(2,1)S(1)}, bf16[192,256]{1,0:T(8,128)(2,1)S(1)}, u32[]{:S(2)}, u32[]{:S(2)}) collective-permute-start(bf16[192,256]{1,0:T(8,128)(2,1)S(1)} %collective-permute-done.8.refs_2_), channel_id=1, source_target_pairs={{0,4},{4,0},{8,12},{12,8},{16,20},{20,16},{24,28},{28,24},{1,5},{5... | collective-permute-start | bytes 294920 | tf_op jit(solution)/shard_map/ppermute | solution.py:224
  42.9 3.0 %collective-permute-done.11.refs_5_ = bf16[192,256]{1,0:T(8,128)(2,1)S(1)} collective-permute-done((bf16[192,256]{1,0:T(8,128)(2,1)S(1)}, bf16[192,256]{1,0:T(8,128)(2,1)S(1)}, u32[]{:S(2)}, u32[]{:S(2)}) %collective-permute-start.11) | collective-permute-done | bytes 98336 | tf_op jit(solution)/shard_map/ppermute | solution.py:224
  45.9 1.1 %collective-permute-done.9.refs_3_ = bf16[192,256]{1,0:T(8,128)(2,1)S(1)} collective-permute-done((bf16[192,256]{1,0:T(8,128)(2,1)S(1)}, bf16[192,256]{1,0:T(8,128)(2,1)S(1)}, u32[]{:S(2)}, u32[]{:S(2)}) %collective-permute-start.9) | collective-permute-done | bytes 98336 | tf_op jit(solution)/shard_map/ppermute | solution.py:224
  47.0 1.1 %shard_map.78 = (bf16[48,1024]{1,0:T(8,128)(2,1)S(1)}, bf16[48,1024]{1,0:T(8,128)(2,1)S(1)}, bf16[48,1024]{1,0:T(8,128)(2,1)S(1)}, bf16[48,1024]{1,0:T(8,128)(2,1)S(1)}) custom-call(bf16[192,256]{1,0:T(8,128)(2,1)S(1)} %shard_map.77.refs_0_, bf16[192,256]{1,0:T(8,128)(2,1)S(1)} %collective-permute-done.7.refs_1_, ...), custom_call_target="tpu_custom_call" | custom-call | tf_op jit(solution)/shard_map/pallas_call | solution.py:284
  48.2 1.6 %collective-permute-start.15 = (bf16[48,1024]{1,0:T(8,128)(2,1)S(1)}, bf16[48,1024]{1,0:T(8,128)(2,1)S(1)}, u32[]{:S(2)}, u32[]{:S(2)}) collective-permute-start(bf16[48,1024]{1,0:T(8,128)(2,1)S(1)} %get-tuple-element.27), channel_id=1, source_target_pairs={{0,2},{1,3},{2,0},{3,1},{4,6},{5,7},{6,4},{7,5},{8,10},{9,11},{10,... | collective-permute-start | bytes 294920 | tf_op jit(solution)/shard_map/ppermute | solution.py:224
  50.1 3.8 %collective-permute-done.15 = bf16[48,1024]{1,0:T(8,128)(2,1)S(1)} collective-permute-done((bf16[48,1024]{1,0:T(8,128)(2,1)S(1)}, bf16[48,1024]{1,0:T(8,128)(2,1)S(1)}, u32[]{:S(2)}, u32[]{:S(2)}) %collective-permute-start.15) | collective-permute-done | bytes 98336 | tf_op jit(solution)/shard_map/ppermute | solution.py:224
  53.9 1.2 %collective-permute-done.16 = bf16[48,1024]{1,0:T(8,128)(2,1)S(1)} collective-permute-done((bf16[48,1024]{1,0:T(8,128)(2,1)S(1)}, bf16[48,1024]{1,0:T(8,128)(2,1)S(1)}, u32[]{:S(2)}, u32[]{:S(2)}) %collective-permute-start.16) | collective-permute-done | bytes 98336 | tf_op jit(solution)/shard_map/ppermute | solution.py:224
  55.1 0.7 %add_convert_fusion = bf16[48,1024]{1,0:T(8,128)(2,1)} fusion(bf16[48,1024]{1,0:T(8,128)(2,1)S(1)} %collective-permute-done.16, bf16[48,1024]{1,0:T(8,128)(2,1)S(1)} %collective-permute-done.15, bf16[48,1024]{1,0:T(8,128)(2,1)S(1)} %collective-permute-done.14, bf16[48,1024]{1,0:T(8,128)(2,1)S(1)} %get-tuple-element.25), kind=kLoop, calls=%fused_computation | loop fusion | flops 393216 | bytes 491520 | tf_op jit(solution)/shard_map/convert_element_type | solution.py:298
  (19 shorter events, 2.0 us)
Async XLA Ops:
  0.0 47.0 %copy-start = (bf16[2048,1024]{1,0:T(8,128)(2,1)S(1)}, bf16[2048,1024]{1,0:T(8,128)(2,1)}, u32[]{:S(2)}) copy-start(bf16[2048,1024]{1,0:T(8,128)(2,1)} %refs_8_.1) | copy-start | bytes 12582916
  11.0 6.8 %collective-permute-start.1 = (bf16[208,256]{1,0:T(8,128)(2,1)S(1)}, bf16[208,256]{1,0:T(8,128)(2,1)S(1)}, u32[]{:S(2)}, u32[]{:S(2)}) collective-permute-start(bf16[208,256]{1,0:T(8,128)(2,1)S(1)} %get-tuple-element.20), channel_id=1, source_target_pairs={{0,4},{4,0},{8,12},{12,8},{16,20},{20,16},{24,28},{28,24},{1,5},{5... | collective-permute-start | bytes 319496 | tf_op jit(solution)/shard_map/ppermute | solution.py:224
  14.0 7.4 %collective-permute-start.3 = (bf16[208,256]{1,0:T(8,128)(2,1)S(1)}, bf16[208,256]{1,0:T(8,128)(2,1)S(1)}, u32[]{:S(2)}, u32[]{:S(2)}) collective-permute-start(bf16[208,256]{1,0:T(8,128)(2,1)S(1)} %get-tuple-element.22), channel_id=1, source_target_pairs={{0,4},{4,0},{8,12},{12,8},{16,20},{20,16},{24,28},{28,24},{1,5},{5... | collective-permute-start | bytes 319496 | tf_op jit(solution)/shard_map/ppermute | solution.py:224
  14.1 10.4 %collective-permute-start.5 = (bf16[208,256]{1,0:T(8,128)(2,1)S(1)}, bf16[208,256]{1,0:T(8,128)(2,1)S(1)}, u32[]{:S(2)}, u32[]{:S(2)}) collective-permute-start(bf16[208,256]{1,0:T(8,128)(2,1)S(1)} %get-tuple-element.24), channel_id=1, source_target_pairs={{0,4},{4,0},{8,12},{12,8},{16,20},{20,16},{24,28},{28,24},{1,5},{5... | collective-permute-start | bytes 319496 | tf_op jit(solution)/shard_map/ppermute | solution.py:224
  16.1 8.9 %collective-permute-start = (bf16[208,256]{1,0:T(8,128)(2,1)S(1)}, bf16[208,256]{1,0:T(8,128)(2,1)S(1)}, u32[]{:S(2)}, u32[]{:S(2)}) collective-permute-start(bf16[208,256]{1,0:T(8,128)(2,1)S(1)} %get-tuple-element.18), channel_id=1, source_target_pairs={{0,4},{4,0},{8,12},{12,8},{16,20},{20,16},{24,28},{28,24},{1,5},{5... | collective-permute-start | bytes 319496 | tf_op jit(solution)/shard_map/ppermute | solution.py:224
  18.1 9.1 %collective-permute-start.2 = (bf16[208,256]{1,0:T(8,128)(2,1)S(1)}, bf16[208,256]{1,0:T(8,128)(2,1)S(1)}, u32[]{:S(2)}, u32[]{:S(2)}) collective-permute-start(bf16[208,256]{1,0:T(8,128)(2,1)S(1)} %shard_map.74), channel_id=1, source_target_pairs={{0,16},{4,20},{8,24},{12,28},{16,0},{20,4},{24,8},{28,12},{1,17},{... | collective-permute-start | bytes 319496 | tf_op jit(solution)/shard_map/ppermute | solution.py:224
  21.7 6.7 %collective-permute-start.4 = (bf16[208,256]{1,0:T(8,128)(2,1)S(1)}, bf16[208,256]{1,0:T(8,128)(2,1)S(1)}, u32[]{:S(2)}, u32[]{:S(2)}) collective-permute-start(bf16[208,256]{1,0:T(8,128)(2,1)S(1)} %shard_map.75), channel_id=1, source_target_pairs={{0,24},{4,28},{8,16},{12,20},{16,8},{20,12},{24,0},{28,4},{1,25},{... | collective-permute-start | bytes 319496 | tf_op jit(solution)/shard_map/ppermute | solution.py:224
  24.8 4.8 %collective-permute-start.6 = (bf16[208,256]{1,0:T(8,128)(2,1)S(1)}, bf16[208,256]{1,0:T(8,128)(2,1)S(1)}, u32[]{:S(2)}, u32[]{:S(2)}) collective-permute-start(bf16[208,256]{1,0:T(8,128)(2,1)S(1)} %shard_map.76), channel_id=1, source_target_pairs={{0,8},{4,12},{8,0},{12,4},{16,24},{20,28},{24,16},{28,20},{1,9},{5... | collective-permute-start | bytes 319496 | tf_op jit(solution)/shard_map/ppermute | solution.py:224
  30.1 6.8 %collective-permute-start.12 = (bf16[192,256]{1,0:T(8,128)(2,1)S(1)}, bf16[192,256]{1,0:T(8,128)(2,1)S(1)}, u32[]{:S(2)}, u32[]{:S(2)}) collective-permute-start(bf16[192,256]{1,0:T(8,128)(2,1)S(1)} %shard_map.77.refs_0_), channel_id=1, source_target_pairs={{0,24},{4,28},{8,16},{12,20},{16,8},{20,12},{24,0},{28,4},{1,25},{... | collective-permute-start | bytes 294920 | tf_op jit(solution)/shard_map/ppermute | solution.py:224
  33.4 7.5 %collective-permute-start.10 = (bf16[192,256]{1,0:T(8,128)(2,1)S(1)}, bf16[192,256]{1,0:T(8,128)(2,1)S(1)}, u32[]{:S(2)}, u32[]{:S(2)}) collective-permute-start(bf16[192,256]{1,0:T(8,128)(2,1)S(1)} %shard_map.77.refs_0_), channel_id=1, source_target_pairs={{0,16},{4,20},{8,24},{12,28},{16,0},{20,4},{24,8},{28,12},{1,17},{... | collective-permute-start | bytes 294920 | tf_op jit(solution)/shard_map/ppermute | solution.py:224
  33.4 8.9 %collective-permute-start.8 = (bf16[192,256]{1,0:T(8,128)(2,1)S(1)}, bf16[192,256]{1,0:T(8,128)(2,1)S(1)}, u32[]{:S(2)}, u32[]{:S(2)}) collective-permute-start(bf16[192,256]{1,0:T(8,128)(2,1)S(1)} %shard_map.77.refs_0_), channel_id=1, source_target_pairs={{0,8},{4,12},{8,0},{12,4},{16,24},{20,28},{24,16},{28,20},{1,9},{5... | collective-permute-start | bytes 294920 | tf_op jit(solution)/shard_map/ppermute | solution.py:224
  34.5 8.4 %collective-permute-start.7 = (bf16[192,256]{1,0:T(8,128)(2,1)S(1)}, bf16[192,256]{1,0:T(8,128)(2,1)S(1)}, u32[]{:S(2)}, u32[]{:S(2)}) collective-permute-start(bf16[192,256]{1,0:T(8,128)(2,1)S(1)} %shard_map.77.refs_0_), channel_id=1, source_target_pairs={{0,4},{4,0},{8,12},{12,8},{16,20},{20,16},{24,28},{28,24},{1,5},{5... | collective-permute-start | bytes 294920 | tf_op jit(solution)/shard_map/ppermute | solution.py:224
  36.8 6.1 %collective-permute-start.13 = (bf16[192,256]{1,0:T(8,128)(2,1)S(1)}, bf16[192,256]{1,0:T(8,128)(2,1)S(1)}, u32[]{:S(2)}, u32[]{:S(2)}) collective-permute-start(bf16[192,256]{1,0:T(8,128)(2,1)S(1)} %collective-permute-done.12.refs_6_), channel_id=1, source_target_pairs={{0,4},{4,0},{8,12},{12,8},{16,20},{20,16},{24,28},{28,24},{1,5},{5... | collective-permute-start | bytes 294920 | tf_op jit(solution)/shard_map/ppermute | solution.py:224
  40.9 5.1 %collective-permute-start.11 = (bf16[192,256]{1,0:T(8,128)(2,1)S(1)}, bf16[192,256]{1,0:T(8,128)(2,1)S(1)}, u32[]{:S(2)}, u32[]{:S(2)}) collective-permute-start(bf16[192,256]{1,0:T(8,128)(2,1)S(1)} %collective-permute-done.10.refs_4_), channel_id=1, source_target_pairs={{0,4},{4,0},{8,12},{12,8},{16,20},{20,16},{24,28},{28,24},{1,5},{5... | collective-permute-start | bytes 294920 | tf_op jit(solution)/shard_map/ppermute | solution.py:224
  42.3 4.7 %collective-permute-start.9 = (bf16[192,256]{1,0:T(8,128)(2,1)S(1)}, bf16[192,256]{1,0:T(8,128)(2,1)S(1)}, u32[]{:S(2)}, u32[]{:S(2)}) collective-permute-start(bf16[192,256]{1,0:T(8,128)(2,1)S(1)} %collective-permute-done.8.refs_2_), channel_id=1, source_target_pairs={{0,4},{4,0},{8,12},{12,8},{16,20},{20,16},{24,28},{28,24},{1,5},{5... | collective-permute-start | bytes 294920 | tf_op jit(solution)/shard_map/ppermute | solution.py:224
  48.1 1.9 %collective-permute-start.14 = (bf16[48,1024]{1,0:T(8,128)(2,1)S(1)}, bf16[48,1024]{1,0:T(8,128)(2,1)S(1)}, u32[]{:S(2)}, u32[]{:S(2)}) collective-permute-start(bf16[48,1024]{1,0:T(8,128)(2,1)S(1)} %get-tuple-element.26), channel_id=1, source_target_pairs={{0,1},{1,0},{2,3},{3,2},{4,5},{5,4},{6,7},{7,6},{8,9},{9,8},{10,11... | collective-permute-start | bytes 294920 | tf_op jit(solution)/shard_map/ppermute | solution.py:224
  48.2 5.7 %collective-permute-start.15 = (bf16[48,1024]{1,0:T(8,128)(2,1)S(1)}, bf16[48,1024]{1,0:T(8,128)(2,1)S(1)}, u32[]{:S(2)}, u32[]{:S(2)}) collective-permute-start(bf16[48,1024]{1,0:T(8,128)(2,1)S(1)} %get-tuple-element.27), channel_id=1, source_target_pairs={{0,2},{1,3},{2,0},{3,1},{4,6},{5,7},{6,4},{7,5},{8,10},{9,11},{10,... | collective-permute-start | bytes 294920 | tf_op jit(solution)/shard_map/ppermute | solution.py:224
  49.8 5.3 %collective-permute-start.16 = (bf16[48,1024]{1,0:T(8,128)(2,1)S(1)}, bf16[48,1024]{1,0:T(8,128)(2,1)S(1)}, u32[]{:S(2)}, u32[]{:S(2)}) collective-permute-start(bf16[48,1024]{1,0:T(8,128)(2,1)S(1)} %get-tuple-element.28), channel_id=1, source_target_pairs={{0,3},{1,2},{2,1},{3,0},{4,7},{5,6},{6,5},{7,4},{8,11},{9,10},{10,... | collective-permute-start | bytes 294920 | tf_op jit(solution)/shard_map/ppermute | solution.py:224

commit v3 on v2

--- a/solution.py
+++ b/solution.py
@@ -86,6 +86,7 @@
                         - lax.broadcasted_iota(jnp.int32, (rows, page_len), 0) % DRAFT
                     )
                     scores = jnp.where(offset <= last, scores, FLOOR)
+                scores = scores * scale
                 raw[s, h] = scores
                 high = functools.reduce(
                     jnp.maximum, [scores[:, i : i + LANES] for i in range(0, page_len, LANES)]
@@ -111,12 +112,17 @@
         def _():
             score(i * CHUNK, False)
 
-    @pl.loop(0, requests)
-    def _(r):
-        for h in range(kv_local):
-            top[r, h] = jnp.broadcast_to(
-                jnp.max(top[r, h], axis=1, keepdims=True), (rows, LANES)
-            )
+    batch = math.gcd(requests, 4)
+
+    @pl.loop(0, requests // batch)
+    def _(i):
+        highs = [
+            (i * batch + b, h, jnp.max(top[i * batch + b, h], axis=1, keepdims=True))
+            for b in range(batch)
+            for h in range(kv_local)
+        ]
+        for r, h, high in highs:
+            top[r, h] = jnp.broadcast_to(high, (rows, LANES))
 
     @pl.loop(0, chunks)
     def _(i):
@@ -128,7 +134,7 @@
                 high = top[r, h]
                 weights = jnp.concatenate(
                     [
-                        jnp.exp2((raw[s, h, :, i : i + LANES] - high) * scale).astype(jnp.bfloat16)
+                        jnp.exp2(raw[s, h, :, i : i + LANES] - high).astype(jnp.bfloat16)
                         for i in range(0, page_len, LANES)
                     ],
                     axis=1,
@@ -166,7 +172,7 @@
                 tops = jnp.where(lane == t, m, tops)
                 sums = jnp.where(lane == t, l, sums)
         tops_sent = tops.astype(jnp.bfloat16).astype(jnp.float32)
-        sums = jnp.where(tops > 0.5 * FLOOR, sums * jnp.exp2((tops - tops_sent) * scale), 0.0)
+        sums = jnp.where(tops > 0.1 * scale * FLOOR, sums * jnp.exp2(tops - tops_sent), 0.0)
         sums_high = sums.astype(jnp.bfloat16).astype(jnp.float32)
         msgs[d][per * DRAFT :, :] = jnp.concatenate(
             [x[:, :group] for x in (tops_sent, sums_high, sums - sums_high, sums)], axis=1
@@ -184,7 +190,7 @@
         tops.append(stat[:, :group])
         masses.append(stat[:, group : 2 * group] + stat[:, 2 * group : 3 * group])
     best = functools.reduce(jnp.maximum, tops)
-    shares = [l * jnp.exp2((m - best) * scale) for m, l in zip(tops, masses)]
+    shares = [l * jnp.exp2(m - best) for m, l in zip(tops, masses)]
     total = functools.reduce(jnp.add, shares)
     inverse = 1.0 / jnp.where(total > 0, total, 1.0)
     shares = [s * inverse for s in shares]
@@ -201,13 +207,14 @@
         out[rows:, :] = jnp.concatenate([best, high, total - high, total], axis=1).astype(jnp.bfloat16)
 
 
-def project_kernel(n_ctx, n_kvh, tg, *refs):
+def project_kernel(order, n_kvh, tg, *refs):
+    n_ctx = len(order)
     parts, w_ref = refs[:n_ctx], refs[n_ctx]
     outs = refs[n_ctx + 1 : n_ctx + 1 + n_kvh]
     a_buf, total = refs[n_ctx + 1 + n_kvh :]
     rows, width = parts[0].shape
     me = lax.axis_index("ctx")
-    for d, p in enumerate(parts):
+    for d, p in zip(order, parts):
         source = me ^ d
         a_buf[
             pl.ds(pl.multiple_of(source % tg * rows, rows), rows),
@@ -270,19 +277,27 @@
             compiler_params=small,
         )(*parts)
 
-    across = sorted(range(0, n_ctx, 2), key=lambda d: (d == 0, d < 4, d))
-    beside = {d: exchange(msgs[d + 1], "ctx", 1) for d in across}
-    got = [exchange(combine([msgs[d], beside[d]], False), "ctx", d) for d in across[:-1]]
-    attended = combine([msgs[0], beside[0], *got], True)
-    every = {0: attended}
-    for d in sorted(range(2, n_ctx, 2), key=lambda d: (d < 4, d)):
-        every[d] = exchange(attended, "ctx", d)
-    for d in sorted(range(0, n_ctx, 2), key=lambda d: (d != 0, d < 4, d)):
+    near = [d for d in (2,) if d < n_ctx]
+    far = sorted(range(4, n_ctx, 2))
+    straight = [1, *near, *(d + 1 for d in near)]
+    beside = {d: exchange(msgs[d + 1], "ctx", 1) for d in far}
+    merged = [combine([msgs[d], beside[d]], False) for d in far]
+    msgs = dict(enumerate(msgs))
+    late = straight[1:]
+    if late and far:
+        held = lax.optimization_barrier((*(msgs[d] for d in late), merged[-1]))
+        msgs.update(zip(late, held))
+    got = [exchange(msgs[d], "ctx", d) for d in straight]
+    got += [exchange(m, "ctx", d) for m, d in zip(merged, far)]
+    attended = combine([msgs[0], *got], True)
+    every = {d: exchange(attended, "ctx", d) for d in [*straight, *far]}
+    for d in far:
         every[d + 1] = exchange(every[d], "ctx", 1)
-    every = [every[d] for d in range(n_ctx)]
+    every[0] = attended
+    order = [0, *straight, *(d + side for d in reversed(far) for side in (0, 1))]
     columns = out_weight.shape[1]
     partial = pl.pallas_call(
-        functools.partial(project_kernel, n_ctx, n_kvh, tg),
+        functools.partial(project_kernel, order, n_kvh, tg),
         out_shape=[jax.ShapeDtypeStruct((tokens // n_kvh, columns), jnp.bfloat16)] * n_kvh,
         in_specs=[vmem] * (n_ctx + 1),
         out_specs=[vmem] * n_kvh,
@@ -291,7 +306,7 @@
             pltpu.VMEM((tokens, columns), jnp.float32),
         ],
         compiler_params=small,
-    )(*every, out_weight)
+    )(*(every[d] for d in order), out_weight)
     sums = partial[0].astype(jnp.float32)
     for d in range(1, n_kvh):
         sums = sums + exchange(partial[d], "kvh", d).astype(jnp.float32)

time: 55.9 us -> 52.8 us (0.945)
  starting transfers between devices: 22.9 us -> 21.5 us
  Pallas kernels: 13.5 us -> 12.5 us
  waiting for transfers between devices: 18.7 us -> 18.1 us
    ppermute x17, starting transfers between devices: 22.9 us -> 21.5 us  [exchange(): lax.ppermute(x, axis, [(i, i ^ d) for i in range(lax.axis_size(axis))])]
    pallas_call x1, Pallas kernels: 11 us -> 10.3 us  [per_device(): pl.pallas_call(functools.partial(attention_kernel, n_ctx, hps, tg), out_s...]
    ppermute x17, waiting for transfers between devices: 18.7 us -> 18.1 us  [exchange(): lax.ppermute(x, axis, [(i, i ^ d) for i in range(lax.axis_size(axis))])]
    pallas_call x4 -> x3, Pallas kernels: 1.35 us -> 1.11 us  [combine(): pl.pallas_call(functools.partial(combine_kernel, final, scale), out_shape...]
  transfers between devices with their start and end apart: 17 -> 17, of which waited for: 10 -> 11; matrix products, arithmetic and copies ran while one was open for 0% -> 0% of each run, Pallas kernels for 2% -> 1%
where the time goes in v3:
time: 52.8 us; the launch traced here: 52.9 us
  starting transfers between devices  21.5 us (41%)
  waiting for transfers between devices  18.1 us (34%)
  Pallas kernels  12.5 us (24%)
  other arithmetic  0.69 us (1%)
    ppermute x17, starting transfers between devices, exchange(): lax.ppermute(x, axis, [(i, i ^ d) for i in range(lax.axis_size(axis))])  21.5 us
    ppermute x17, waiting for transfers between devices, exchange(): lax.ppermute(x, axis, [(i, i ^ d) for i in range(lax.axis_size(axis))])  18.1 us
    pallas_call x1, Pallas kernels, per_device(): pl.pallas_call(functools.partial(attention_kernel, n_ctx, hps, tg), out_s...  10.3 us
    pallas_call x1, Pallas kernels, per_device(): pl.pallas_call(functools.partial(project_kernel, order, n_kvh, tg), out_s...  1.12 us
    pallas_call x3, Pallas kernels, combine(): pl.pallas_call(functools.partial(combine_kernel, final, scale), out_shape...  1.11 us
  transfers between devices with their start and end apart: 17, of which 11 were waited for; matrix products, arithmetic and copies ran while one was open for 0% of the time, Pallas kernels for 1%

profile of v3, /device:TPU:0, one launch (start us, length us, event | category | flops | bytes accessed | tf_op | source)
XLA Modules:
  0.0 52.9 jit_solution(15226303029851031125)
XLA Ops:
  0.0 10.3 %shard_map.73 = (bf16[208,256]{1,0:T(8,128)(2,1)S(1)}, bf16[208,256]{1,0:T(8,128)(2,1)S(1)}, bf16[208,256]{1,0:T(8,128)(2,1)S(1)}, bf16[208,256]{1,0:T(8,128)(2,...) custom-call(s32[12]{0:T(128)} %len_hbm.1, ...), custom_call_target="tpu_custom_call" | custom-call | tf_op jit(solution)/shard_map/pallas_call | solution.py:248
  10.3 2.8 %collective-permute-start.1 = (bf16[208,256]{1,0:T(8,128)(2,1)S(1)}, bf16[208,256]{1,0:T(8,128)(2,1)S(1)}, u32[]{:S(2)}, u32[]{:S(2)}) collective-permute-start(bf16[208,256]{1,0:T(8,128)(2,1)S(1)} %get-tuple-element.24), channel_id=1, source_target_pairs={{0,4},{4,0},{8,12},{12,8},{16,20},{20,16},{24,28},{28,24},{1,5},{5... | collective-permute-start | bytes 319496 | tf_op jit(solution)/shard_map/ppermute | solution.py:231
  13.2 1.9 %collective-permute-start = (bf16[208,256]{1,0:T(8,128)(2,1)S(1)}, bf16[208,256]{1,0:T(8,128)(2,1)S(1)}, u32[]{:S(2)}, u32[]{:S(2)}) collective-permute-start(bf16[208,256]{1,0:T(8,128)(2,1)S(1)} %get-tuple-element.20), channel_id=1, source_target_pairs={{0,4},{4,0},{8,12},{12,8},{16,20},{20,16},{24,28},{28,24},{1,5},{5... | collective-permute-start | bytes 319496 | tf_op jit(solution)/shard_map/ppermute | solution.py:231
  15.2 1.8 %collective-permute-done.1.refs_1_ = bf16[208,256]{1,0:T(8,128)(2,1)S(1)} collective-permute-done((bf16[208,256]{1,0:T(8,128)(2,1)S(1)}, bf16[208,256]{1,0:T(8,128)(2,1)S(1)}, u32[]{:S(2)}, u32[]{:S(2)}) %collective-permute-start.1) | collective-permute-done | bytes 106528 | tf_op jit(solution)/shard_map/ppermute | solution.py:231
  17.2 3.8 %collective-permute-start.6 = (bf16[208,256]{1,0:T(8,128)(2,1)S(1)}, bf16[208,256]{1,0:T(8,128)(2,1)S(1)}, u32[]{:S(2)}, u32[]{:S(2)}) collective-permute-start(bf16[208,256]{1,0:T(8,128)(2,1)S(1)} %shard_map.74), channel_id=1, source_target_pairs={{0,24},{4,28},{8,16},{12,20},{16,8},{20,12},{24,0},{28,4},{1,25},{... | collective-permute-start | bytes 319496 | tf_op jit(solution)/shard_map/ppermute | solution.py:231
  21.2 3.4 %collective-permute-start.3 = (bf16[208,256]{1,0:T(8,128)(2,1)S(1)}, bf16[208,256]{1,0:T(8,128)(2,1)S(1)}, u32[]{:S(2)}, u32[]{:S(2)}) collective-permute-start(bf16[208,256]{1,0:T(8,128)(2,1)S(1)} %get-tuple-element.26), channel_id=1, source_target_pairs={{0,12},{4,8},{8,4},{12,0},{16,28},{20,24},{24,20},{28,16},{1,13},{... | collective-permute-start | bytes 319496 | tf_op jit(solution)/shard_map/ppermute | solution.py:231
  25.0 2.3 %collective-permute-done.2.refs_2_ = bf16[208,256]{1,0:T(8,128)(2,1)S(1)} collective-permute-done((bf16[208,256]{1,0:T(8,128)(2,1)S(1)}, bf16[208,256]{1,0:T(8,128)(2,1)S(1)}, u32[]{:S(2)}, u32[]{:S(2)}) %collective-permute-start.2) | collective-permute-done | bytes 106528 | tf_op jit(solution)/shard_map/ppermute | solution.py:231
  27.4 2.4 %collective-permute-done.3.refs_3_ = bf16[208,256]{1,0:T(8,128)(2,1)S(1)} collective-permute-done((bf16[208,256]{1,0:T(8,128)(2,1)S(1)}, bf16[208,256]{1,0:T(8,128)(2,1)S(1)}, u32[]{:S(2)}, u32[]{:S(2)}) %collective-permute-start.3) | collective-permute-done | bytes 106528 | tf_op jit(solution)/shard_map/ppermute | solution.py:231
  29.7 1.5 %collective-permute-done.5.refs_4_ = bf16[208,256]{1,0:T(8,128)(2,1)S(1)} collective-permute-done((bf16[208,256]{1,0:T(8,128)(2,1)S(1)}, bf16[208,256]{1,0:T(8,128)(2,1)S(1)}, u32[]{:S(2)}, u32[]{:S(2)}) %collective-permute-start.5) | collective-permute-done | bytes 106528 | tf_op jit(solution)/shard_map/ppermute | solution.py:231
  31.7 0.9 %collective-permute-start.12 = (bf16[192,256]{1,0:T(8,128)(2,1)S(1)}, bf16[192,256]{1,0:T(8,128)(2,1)S(1)}, u32[]{:S(2)}, u32[]{:S(2)}) collective-permute-start(bf16[192,256]{1,0:T(8,128)(2,1)S(1)} %shard_map.76.refs_0_), channel_id=1, source_target_pairs={{0,16},{4,20},{8,24},{12,28},{16,0},{20,4},{24,8},{28,12},{1,17},{... | collective-permute-start | bytes 294920 | tf_op jit(solution)/shard_map/ppermute | solution.py:231
  32.6 1.1 %collective-permute-start.10 = (bf16[192,256]{1,0:T(8,128)(2,1)S(1)}, bf16[192,256]{1,0:T(8,128)(2,1)S(1)}, u32[]{:S(2)}, u32[]{:S(2)}) collective-permute-start(bf16[192,256]{1,0:T(8,128)(2,1)S(1)} %shard_map.76.refs_0_), channel_id=1, source_target_pairs={{0,24},{4,28},{8,16},{12,20},{16,8},{20,12},{24,0},{28,4},{1,25},{... | collective-permute-start | bytes 294920 | tf_op jit(solution)/shard_map/ppermute | solution.py:231
  33.7 1.5 %collective-permute-start.9 = (bf16[192,256]{1,0:T(8,128)(2,1)S(1)}, bf16[192,256]{1,0:T(8,128)(2,1)S(1)}, u32[]{:S(2)}, u32[]{:S(2)}) collective-permute-start(bf16[192,256]{1,0:T(8,128)(2,1)S(1)} %shard_map.76.refs_0_), channel_id=1, source_target_pairs={{0,12},{4,8},{8,4},{12,0},{16,28},{20,24},{24,20},{28,16},{1,13},{... | collective-permute-start | bytes 294920 | tf_op jit(solution)/shard_map/ppermute | solution.py:231
  35.9 1.3 %collective-permute-start.7 = (bf16[192,256]{1,0:T(8,128)(2,1)S(1)}, bf16[192,256]{1,0:T(8,128)(2,1)S(1)}, u32[]{:S(2)}, u32[]{:S(2)}) collective-permute-start(bf16[192,256]{1,0:T(8,128)(2,1)S(1)} %shard_map.76.refs_0_), channel_id=1, source_target_pairs={{0,4},{4,0},{8,12},{12,8},{16,20},{20,16},{24,28},{28,24},{1,5},{5... | collective-permute-start | bytes 294920 | tf_op jit(solution)/shard_map/ppermute | solution.py:231
  37.2 0.7 %collective-permute-done.12.refs_6_ = bf16[192,256]{1,0:T(8,128)(2,1)S(1)} collective-permute-done((bf16[192,256]{1,0:T(8,128)(2,1)S(1)}, bf16[192,256]{1,0:T(8,128)(2,1)S(1)}, u32[]{:S(2)}, u32[]{:S(2)}) %collective-permute-start.12) | collective-permute-done | bytes 98336 | tf_op jit(solution)/shard_map/ppermute | solution.py:231
  37.9 0.8 %collective-permute-start.13 = (bf16[192,256]{1,0:T(8,128)(2,1)S(1)}, bf16[192,256]{1,0:T(8,128)(2,1)S(1)}, u32[]{:S(2)}, u32[]{:S(2)}) collective-permute-start(bf16[192,256]{1,0:T(8,128)(2,1)S(1)} %collective-permute-done.12.refs_6_), channel_id=1, source_target_pairs={{0,4},{4,0},{8,12},{12,8},{16,20},{20,16},{24,28},{28,24},{1,5},{5... | collective-permute-start | bytes 294920 | tf_op jit(solution)/shard_map/ppermute | solution.py:231
  38.7 0.8 %collective-permute-done.10.refs_4_ = bf16[192,256]{1,0:T(8,128)(2,1)S(1)} collective-permute-done((bf16[192,256]{1,0:T(8,128)(2,1)S(1)}, bf16[192,256]{1,0:T(8,128)(2,1)S(1)}, u32[]{:S(2)}, u32[]{:S(2)}) %collective-permute-start.10) | collective-permute-done | bytes 98336 | tf_op jit(solution)/shard_map/ppermute | solution.py:231
  39.5 1.0 %collective-permute-start.11 = (bf16[192,256]{1,0:T(8,128)(2,1)S(1)}, bf16[192,256]{1,0:T(8,128)(2,1)S(1)}, u32[]{:S(2)}, u32[]{:S(2)}) collective-permute-start(bf16[192,256]{1,0:T(8,128)(2,1)S(1)} %collective-permute-done.10.refs_4_), channel_id=1, source_target_pairs={{0,4},{4,0},{8,12},{12,8},{16,20},{20,16},{24,28},{28,24},{1,5},{5... | collective-permute-start | bytes 294920 | tf_op jit(solution)/shard_map/ppermute | solution.py:231
  41.0 1.5 %collective-permute-done.13.refs_7_ = bf16[192,256]{1,0:T(8,128)(2,1)S(1)} collective-permute-done((bf16[192,256]{1,0:T(8,128)(2,1)S(1)}, bf16[192,256]{1,0:T(8,128)(2,1)S(1)}, u32[]{:S(2)}, u32[]{:S(2)}) %collective-permute-start.13) | collective-permute-done | bytes 98336 | tf_op jit(solution)/shard_map/ppermute | solution.py:231
  42.5 1.6 %collective-permute-done.11.refs_5_ = bf16[192,256]{1,0:T(8,128)(2,1)S(1)} collective-permute-done((bf16[192,256]{1,0:T(8,128)(2,1)S(1)}, bf16[192,256]{1,0:T(8,128)(2,1)S(1)}, u32[]{:S(2)}, u32[]{:S(2)}) %collective-permute-start.11) | collective-permute-done | bytes 98336 | tf_op jit(solution)/shard_map/ppermute | solution.py:231
  44.1 1.1 %shard_map.77 = (bf16[48,1024]{1,0:T(8,128)(2,1)S(1)}, bf16[48,1024]{1,0:T(8,128)(2,1)S(1)}, bf16[48,1024]{1,0:T(8,128)(2,1)S(1)}, bf16[48,1024]{1,0:T(8,128)(2,1)S(1)}) custom-call(bf16[192,256]{1,0:T(8,128)(2,1)S(1)} %shard_map.76.refs_0_, bf16[192,256]{1,0:T(8,128)(2,1)S(1)} %collective-permute-done.7.refs_1_, ...), custom_call_target="tpu_custom_call" | custom-call | tf_op jit(solution)/shard_map/pallas_call | solution.py:299
  45.3 1.6 %collective-permute-start.15 = (bf16[48,1024]{1,0:T(8,128)(2,1)S(1)}, bf16[48,1024]{1,0:T(8,128)(2,1)S(1)}, u32[]{:S(2)}, u32[]{:S(2)}) collective-permute-start(bf16[48,1024]{1,0:T(8,128)(2,1)S(1)} %get-tuple-element.31), channel_id=1, source_target_pairs={{0,2},{1,3},{2,0},{3,1},{4,6},{5,7},{6,4},{7,5},{8,10},{9,11},{10,... | collective-permute-start | bytes 294920 | tf_op jit(solution)/shard_map/ppermute | solution.py:231
  47.2 3.8 %collective-permute-done.15 = bf16[48,1024]{1,0:T(8,128)(2,1)S(1)} collective-permute-done((bf16[48,1024]{1,0:T(8,128)(2,1)S(1)}, bf16[48,1024]{1,0:T(8,128)(2,1)S(1)}, u32[]{:S(2)}, u32[]{:S(2)}) %collective-permute-start.15) | collective-permute-done | bytes 98336 | tf_op jit(solution)/shard_map/ppermute | solution.py:231
  51.0 1.2 %collective-permute-done.16 = bf16[48,1024]{1,0:T(8,128)(2,1)S(1)} collective-permute-done((bf16[48,1024]{1,0:T(8,128)(2,1)S(1)}, bf16[48,1024]{1,0:T(8,128)(2,1)S(1)}, u32[]{:S(2)}, u32[]{:S(2)}) %collective-permute-start.16) | collective-permute-done | bytes 98336 | tf_op jit(solution)/shard_map/ppermute | solution.py:231
  52.2 0.7 %add_convert_fusion = bf16[48,1024]{1,0:T(8,128)(2,1)} fusion(bf16[48,1024]{1,0:T(8,128)(2,1)S(1)} %collective-permute-done.16, bf16[48,1024]{1,0:T(8,128)(2,1)S(1)} %collective-permute-done.15, bf16[48,1024]{1,0:T(8,128)(2,1)S(1)} %collective-permute-done.14, bf16[48,1024]{1,0:T(8,128)(2,1)S(1)} %get-tuple-element.29), kind=kLoop, calls=%fused_computation | loop fusion | flops 393216 | bytes 491520 | tf_op jit(solution)/shard_map/convert_element_type | solution.py:313
  (18 shorter events, 3.0 us)
Async XLA Ops:
  0.0 44.1 %copy-start = (bf16[2048,1024]{1,0:T(8,128)(2,1)S(1)}, bf16[2048,1024]{1,0:T(8,128)(2,1)}, u32[]{:S(2)}) copy-start(bf16[2048,1024]{1,0:T(8,128)(2,1)} %refs_8_.1) | copy-start | bytes 12582916
  10.3 6.6 %collective-permute-start.1 = (bf16[208,256]{1,0:T(8,128)(2,1)S(1)}, bf16[208,256]{1,0:T(8,128)(2,1)S(1)}, u32[]{:S(2)}, u32[]{:S(2)}) collective-permute-start(bf16[208,256]{1,0:T(8,128)(2,1)S(1)} %get-tuple-element.24), channel_id=1, source_target_pairs={{0,4},{4,0},{8,12},{12,8},{16,20},{20,16},{24,28},{28,24},{1,5},{5... | collective-permute-start | bytes 319496 | tf_op jit(solution)/shard_map/ppermute | solution.py:231
  13.1 11.5 %collective-permute-start.4 = (bf16[208,256]{1,0:T(8,128)(2,1)S(1)}, bf16[208,256]{1,0:T(8,128)(2,1)S(1)}, u32[]{:S(2)}, u32[]{:S(2)}) collective-permute-start(bf16[208,256]{1,0:T(8,128)(2,1)S(1)} %get-tuple-element.28), channel_id=1, source_target_pairs={{0,4},{4,0},{8,12},{12,8},{16,20},{20,16},{24,28},{28,24},{1,5},{5... | collective-permute-start | bytes 319496 | tf_op jit(solution)/shard_map/ppermute | solution.py:231
  13.2 11.8 %collective-permute-start = (bf16[208,256]{1,0:T(8,128)(2,1)S(1)}, bf16[208,256]{1,0:T(8,128)(2,1)S(1)}, u32[]{:S(2)}, u32[]{:S(2)}) collective-permute-start(bf16[208,256]{1,0:T(8,128)(2,1)S(1)} %get-tuple-element.20), channel_id=1, source_target_pairs={{0,4},{4,0},{8,12},{12,8},{16,20},{20,16},{24,28},{28,24},{1,5},{5... | collective-permute-start | bytes 319496 | tf_op jit(solution)/shard_map/ppermute | solution.py:231
  17.2 12.5 %collective-permute-start.6 = (bf16[208,256]{1,0:T(8,128)(2,1)S(1)}, bf16[208,256]{1,0:T(8,128)(2,1)S(1)}, u32[]{:S(2)}, u32[]{:S(2)}) collective-permute-start(bf16[208,256]{1,0:T(8,128)(2,1)S(1)} %shard_map.74), channel_id=1, source_target_pairs={{0,24},{4,28},{8,16},{12,20},{16,8},{20,12},{24,0},{28,4},{1,25},{... | collective-permute-start | bytes 319496 | tf_op jit(solution)/shard_map/ppermute | solution.py:231
  21.1 6.3 %collective-permute-start.2 = (bf16[208,256]{1,0:T(8,128)(2,1)S(1)}, bf16[208,256]{1,0:T(8,128)(2,1)S(1)}, u32[]{:S(2)}, u32[]{:S(2)}) collective-permute-start(bf16[208,256]{1,0:T(8,128)(2,1)S(1)} %get-tuple-element.25), channel_id=1, source_target_pairs={{0,8},{4,12},{8,0},{12,4},{16,24},{20,28},{24,16},{28,20},{1,9},{5... | collective-permute-start | bytes 319496 | tf_op jit(solution)/shard_map/ppermute | solution.py:231
  21.2 8.5 %collective-permute-start.3 = (bf16[208,256]{1,0:T(8,128)(2,1)S(1)}, bf16[208,256]{1,0:T(8,128)(2,1)S(1)}, u32[]{:S(2)}, u32[]{:S(2)}) collective-permute-start(bf16[208,256]{1,0:T(8,128)(2,1)S(1)} %get-tuple-element.26), channel_id=1, source_target_pairs={{0,12},{4,8},{8,4},{12,0},{16,28},{20,24},{24,20},{28,16},{1,13},{... | collective-permute-start | bytes 319496 | tf_op jit(solution)/shard_map/ppermute | solution.py:231
  24.9 6.3 %collective-permute-start.5 = (bf16[208,256]{1,0:T(8,128)(2,1)S(1)}, bf16[208,256]{1,0:T(8,128)(2,1)S(1)}, u32[]{:S(2)}, u32[]{:S(2)}) collective-permute-start(bf16[208,256]{1,0:T(8,128)(2,1)S(1)} %shard_map.75), channel_id=1, source_target_pairs={{0,16},{4,20},{8,24},{12,28},{16,0},{20,4},{24,8},{28,12},{1,17},{... | collective-permute-start | bytes 319496 | tf_op jit(solution)/shard_map/ppermute | solution.py:231
  31.7 6.2 %collective-permute-start.12 = (bf16[192,256]{1,0:T(8,128)(2,1)S(1)}, bf16[192,256]{1,0:T(8,128)(2,1)S(1)}, u32[]{:S(2)}, u32[]{:S(2)}) collective-permute-start(bf16[192,256]{1,0:T(8,128)(2,1)S(1)} %shard_map.76.refs_0_), channel_id=1, source_target_pairs={{0,16},{4,20},{8,24},{12,28},{16,0},{20,4},{24,8},{28,12},{1,17},{... | collective-permute-start | bytes 294920 | tf_op jit(solution)/shard_map/ppermute | solution.py:231
  32.6 6.9 %collective-permute-start.10 = (bf16[192,256]{1,0:T(8,128)(2,1)S(1)}, bf16[192,256]{1,0:T(8,128)(2,1)S(1)}, u32[]{:S(2)}, u32[]{:S(2)}) collective-permute-start(bf16[192,256]{1,0:T(8,128)(2,1)S(1)} %shard_map.76.refs_0_), channel_id=1, source_target_pairs={{0,24},{4,28},{8,16},{12,20},{16,8},{20,12},{24,0},{28,4},{1,25},{... | collective-permute-start | bytes 294920 | tf_op jit(solution)/shard_map/ppermute | solution.py:231
  33.7 6.8 %collective-permute-start.9 = (bf16[192,256]{1,0:T(8,128)(2,1)S(1)}, bf16[192,256]{1,0:T(8,128)(2,1)S(1)}, u32[]{:S(2)}, u32[]{:S(2)}) collective-permute-start(bf16[192,256]{1,0:T(8,128)(2,1)S(1)} %shard_map.76.refs_0_), channel_id=1, source_target_pairs={{0,12},{4,8},{8,4},{12,0},{16,28},{20,24},{24,20},{28,16},{1,13},{... | collective-permute-start | bytes 294920 | tf_op jit(solution)/shard_map/ppermute | solution.py:231
  35.2 5.8 %collective-permute-start.8 = (bf16[192,256]{1,0:T(8,128)(2,1)S(1)}, bf16[192,256]{1,0:T(8,128)(2,1)S(1)}, u32[]{:S(2)}, u32[]{:S(2)}) collective-permute-start(bf16[192,256]{1,0:T(8,128)(2,1)S(1)} %shard_map.76.refs_0_), channel_id=1, source_target_pairs={{0,8},{4,12},{8,0},{12,4},{16,24},{20,28},{24,16},{28,20},{1,9},{5... | collective-permute-start | bytes 294920 | tf_op jit(solution)/shard_map/ppermute | solution.py:231
  35.9 5.2 %collective-permute-start.7 = (bf16[192,256]{1,0:T(8,128)(2,1)S(1)}, bf16[192,256]{1,0:T(8,128)(2,1)S(1)}, u32[]{:S(2)}, u32[]{:S(2)}) collective-permute-start(bf16[192,256]{1,0:T(8,128)(2,1)S(1)} %shard_map.76.refs_0_), channel_id=1, source_target_pairs={{0,4},{4,0},{8,12},{12,8},{16,20},{20,16},{24,28},{28,24},{1,5},{5... | collective-permute-start | bytes 294920 | tf_op jit(solution)/shard_map/ppermute | solution.py:231
  37.9 4.6 %collective-permute-start.13 = (bf16[192,256]{1,0:T(8,128)(2,1)S(1)}, bf16[192,256]{1,0:T(8,128)(2,1)S(1)}, u32[]{:S(2)}, u32[]{:S(2)}) collective-permute-start(bf16[192,256]{1,0:T(8,128)(2,1)S(1)} %collective-permute-done.12.refs_6_), channel_id=1, source_target_pairs={{0,4},{4,0},{8,12},{12,8},{16,20},{20,16},{24,28},{28,24},{1,5},{5... | collective-permute-start | bytes 294920 | tf_op jit(solution)/shard_map/ppermute | solution.py:231
  39.5 4.6 %collective-permute-start.11 = (bf16[192,256]{1,0:T(8,128)(2,1)S(1)}, bf16[192,256]{1,0:T(8,128)(2,1)S(1)}, u32[]{:S(2)}, u32[]{:S(2)}) collective-permute-start(bf16[192,256]{1,0:T(8,128)(2,1)S(1)} %collective-permute-done.10.refs_4_), channel_id=1, source_target_pairs={{0,4},{4,0},{8,12},{12,8},{16,20},{20,16},{24,28},{28,24},{1,5},{5... | collective-permute-start | bytes 294920 | tf_op jit(solution)/shard_map/ppermute | solution.py:231
  45.2 1.9 %collective-permute-start.14 = (bf16[48,1024]{1,0:T(8,128)(2,1)S(1)}, bf16[48,1024]{1,0:T(8,128)(2,1)S(1)}, u32[]{:S(2)}, u32[]{:S(2)}) collective-permute-start(bf16[48,1024]{1,0:T(8,128)(2,1)S(1)} %get-tuple-element.30), channel_id=1, source_target_pairs={{0,1},{1,0},{2,3},{3,2},{4,5},{5,4},{6,7},{7,6},{8,9},{9,8},{10,11... | collective-permute-start | bytes 294920 | tf_op jit(solution)/shard_map/ppermute | solution.py:231
  45.3 5.7 %collective-permute-start.15 = (bf16[48,1024]{1,0:T(8,128)(2,1)S(1)}, bf16[48,1024]{1,0:T(8,128)(2,1)S(1)}, u32[]{:S(2)}, u32[]{:S(2)}) collective-permute-start(bf16[48,1024]{1,0:T(8,128)(2,1)S(1)} %get-tuple-element.31), channel_id=1, source_target_pairs={{0,2},{1,3},{2,0},{3,1},{4,6},{5,7},{6,4},{7,5},{8,10},{9,11},{10,... | collective-permute-start | bytes 294920 | tf_op jit(solution)/shard_map/ppermute | solution.py:231
  46.9 5.3 %collective-permute-start.16 = (bf16[48,1024]{1,0:T(8,128)(2,1)S(1)}, bf16[48,1024]{1,0:T(8,128)(2,1)S(1)}, u32[]{:S(2)}, u32[]{:S(2)}) collective-permute-start(bf16[48,1024]{1,0:T(8,128)(2,1)S(1)} %get-tuple-element.32), channel_id=1, source_target_pairs={{0,3},{1,2},{2,1},{3,0},{4,7},{5,6},{6,5},{7,4},{8,11},{9,10},{10,... | collective-permute-start | bytes 294920 | tf_op jit(solution)/shard_map/ppermute | solution.py:231

commit v4 on v3

--- a/solution.py
+++ b/solution.py
@@ -207,24 +207,40 @@
         out[rows:, :] = jnp.concatenate([best, high, total - high, total], axis=1).astype(jnp.bfloat16)
 
 
-def project_kernel(order, n_kvh, tg, *refs):
-    n_ctx = len(order)
-    parts, w_ref = refs[:n_ctx], refs[n_ctx]
-    outs = refs[n_ctx + 1 : n_ctx + 1 + n_kvh]
-    a_buf, total = refs[n_ctx + 1 + n_kvh :]
+def project_kernel(order, n_kvh, tg, first, last, *refs):
+    refs = list(refs)
+    before = None if first else refs.pop(0)
+    parts = [refs.pop(0) for _ in order]
+    w_ref = refs.pop(0)
+    columns = w_ref.shape[1]
     rows, width = parts[0].shape
     me = lax.axis_index("ctx")
-    for d, p in zip(order, parts):
-        source = me ^ d
-        a_buf[
-            pl.ds(pl.multiple_of(source % tg * rows, rows), rows),
-            pl.ds(pl.multiple_of(source // tg * width, width), width),
-        ] = p[...]
-    total[...] = jnp.dot(a_buf[...], w_ref[...], preferred_element_type=jnp.float32)
-    mine = lax.axis_index("kvh")
-    count = outs[0].shape[0]
-    for d, o in enumerate(outs):
-        o[...] = total[pl.ds(pl.multiple_of((mine ^ d) * count, 8), count), :].astype(jnp.bfloat16)
+    if tg == 1:
+        a_buf, w_buf = None, [
+            w_ref.at[pl.ds(pl.multiple_of((me ^ d) * width, width), width)] for d in order
+        ]
+    else:
+        a_buf = refs.pop()
+        for d, p in zip(order, parts):
+            source = me ^ d
+            a_buf[
+                pl.ds(pl.multiple_of(source % tg * rows, rows), rows),
+                pl.ds(pl.multiple_of(source // tg * width, width), width),
+            ] = p[...]
+        parts, w_buf = [a_buf], [w_ref]
+    total = refs.pop()
+    step = math.gcd(columns, 256)
+    for c in range(0, columns, step):
+        at = slice(c, c + step)
+        sums = [jnp.dot(p[...], w[:, at], preferred_element_type=jnp.float32) for p, w in zip(parts, w_buf)]
+        if before is not None:
+            sums.append(before[:, at])
+        total[:, at] = functools.reduce(jnp.add, sums)
+    if last:
+        mine = lax.axis_index("kvh")
+        count = refs[0].shape[0]
+        for d, o in enumerate(refs):
+            o[...] = total[pl.ds(pl.multiple_of((mine ^ d) * count, 8), count), :].astype(jnp.bfloat16)
 
 
 def exchange(x, axis, d):
@@ -277,36 +293,57 @@
             compiler_params=small,
         )(*parts)
 
+    close = [d for d in (1, 2, 3) if d < n_ctx]
+    distant = range(4, n_ctx, 4)
+    pieces = dict(enumerate(msgs))
+    merged = [
+        combine([pieces[e], *(exchange(pieces[e + d], "ctx", d) for d in close)], False)
+        for e in distant
+    ]
+    late = []
+    if late and merged:
+        held = lax.optimization_barrier((*(pieces[d] for d in late), *merged))
+        pieces.update(zip(late, held))
+    got = [exchange(pieces[d], "ctx", d) for d in close]
+    got += [exchange(m, "ctx", e) for m, e in zip(merged, distant)]
+    attended = combine([msgs[0], *got], True)
     near = [d for d in (2,) if d < n_ctx]
     far = sorted(range(4, n_ctx, 2))
     straight = [1, *near, *(d + 1 for d in near)]
-    beside = {d: exchange(msgs[d + 1], "ctx", 1) for d in far}
-    merged = [combine([msgs[d], beside[d]], False) for d in far]
-    msgs = dict(enumerate(msgs))
-    late = straight[1:]
-    if late and far:
-        held = lax.optimization_barrier((*(msgs[d] for d in late), merged[-1]))
-        msgs.update(zip(late, held))
-    got = [exchange(msgs[d], "ctx", d) for d in straight]
-    got += [exchange(m, "ctx", d) for m, d in zip(merged, far)]
-    attended = combine([msgs[0], *got], True)
     every = {d: exchange(attended, "ctx", d) for d in [*straight, *far]}
     for d in far:
         every[d + 1] = exchange(every[d], "ctx", 1)
     every[0] = attended
     order = [0, *straight, *(d + side for d in reversed(far) for side in (0, 1))]
     columns = out_weight.shape[1]
-    partial = pl.pallas_call(
-        functools.partial(project_kernel, order, n_kvh, tg),
-        out_shape=[jax.ShapeDtypeStruct((tokens // n_kvh, columns), jnp.bfloat16)] * n_kvh,
-        in_specs=[vmem] * (n_ctx + 1),
-        out_specs=[vmem] * n_kvh,
-        scratch_shapes=[
-            pltpu.VMEM((tokens, heads * head), jnp.bfloat16),
-            pltpu.VMEM((tokens, columns), jnp.float32),
-        ],
-        compiler_params=small,
-    )(*(every[d] for d in order), out_weight)
+    tail = [d for d in order if d >= 4 and d % 2] if tg == 1 else []
+    head_parts = [d for d in [0, *reversed(straight), *reversed(far)] if d not in tail]
+    tail = tail[::-1]
+
+    def project(ds, first, last, *carry):
+        outs = [jax.ShapeDtypeStruct((tokens // n_kvh, columns), jnp.bfloat16)] * n_kvh
+        whole = jax.ShapeDtypeStruct((tokens, columns), jnp.float32)
+        scratch = [pltpu.VMEM(whole.shape, whole.dtype)] if last else []
+        if tg > 1:
+            scratch.append(pltpu.VMEM((tokens, heads * head), jnp.bfloat16))
+        return pl.pallas_call(
+            functools.partial(project_kernel, ds, n_kvh, tg, first, last),
+            out_shape=outs if last else whole,
+            in_specs=[vmem] * (len(carry) + len(ds) + 1),
+            out_specs=[vmem] * n_kvh if last else vmem,
+            scratch_shapes=scratch,
+            compiler_params=small,
+            cost_estimate=pl.CostEstimate(
+                flops=2 * rows * width * columns * len(ds),
+                bytes_accessed=2 * width * columns * len(ds),
+                transcendentals=0,
+            ),
+        )(*carry, *(every[d] for d in ds), out_weight)
+
+    if tail:
+        partial = project(tail, False, True, project(head_parts, True, False))
+    else:
+        partial = project(order, True, True)
     sums = partial[0].astype(jnp.float32)
     for d in range(1, n_kvh):
         sums = sums + exchange(partial[d], "kvh", d).astype(jnp.float32)

time: 52.8 us -> 51.3 us (0.972)
  waiting for transfers between devices: 18.1 us -> 16.9 us
    ppermute x17, waiting for transfers between devices: 18.1 us -> 16.9 us  [exchange(): lax.ppermute(x, axis, [(i, i ^ d) for i in range(lax.axis_size(axis))])]
    pallas_call x3 -> x2, Pallas kernels: 1.11 us -> 0.87 us  [combine(): pl.pallas_call(functools.partial(combine_kernel, final, scale), out_shape...]
    pallas_call x1 -> x2, Pallas kernels: 1.12 us -> 1.22 us  [project(): pl.pallas_call(functools.partial(project_kernel, ds, n_kvh, tg, first, la...]
  transfers between devices with their start and end apart: 17 -> 17, of which waited for: 11 -> 12; matrix products, arithmetic and copies ran while one was open for 0% -> 0% of each run, Pallas kernels for 1% -> 2%
where the time goes in v4:
time: 51.3 us; the launch traced here: 51 us
  starting transfers between devices  21.3 us (42%)
  waiting for transfers between devices  16.9 us (33%)
  Pallas kernels  12 us (23%)
  other arithmetic  0.69 us (1%)
    ppermute x17, starting transfers between devices, exchange(): lax.ppermute(x, axis, [(i, i ^ d) for i in range(lax.axis_size(axis))])  21.3 us
    ppermute x17, waiting for transfers between devices, exchange(): lax.ppermute(x, axis, [(i, i ^ d) for i in range(lax.axis_size(axis))])  16.9 us
    pallas_call x1, Pallas kernels, per_device(): pl.pallas_call(functools.partial(attention_kernel, n_ctx, hps, tg), out_s...  9.95 us
    pallas_call x2, Pallas kernels, project(): pl.pallas_call(functools.partial(project_kernel, ds, n_kvh, tg, first, la...  1.22 us
  transfers between devices with their start and end apart: 17, of which 12 were waited for; matrix products, arithmetic and copies ran while one was open for 0% of the time, Pallas kernels for 2%

profile of v4, /device:TPU:0, one launch (start us, length us, event | category | flops | bytes accessed | tf_op | source)
XLA Modules:
  0.0 51.0 jit_solution(1464948922706646109)
XLA Ops:
  0.0 9.9 %shard_map.73 = (bf16[208,256]{1,0:T(8,128)(2,1)S(1)}, bf16[208,256]{1,0:T(8,128)(2,1)S(1)}, bf16[208,256]{1,0:T(8,128)(2,1)S(1)}, bf16[208,256]{1,0:T(8,128)(2,...) custom-call(s32[12]{0:T(128)} %len_hbm.1, ...), custom_call_target="tpu_custom_call" | custom-call | tf_op jit(solution)/shard_map/pallas_call | solution.py:264
  10.0 3.2 %collective-permute-start.3 = (bf16[208,256]{1,0:T(8,128)(2,1)S(1)}, bf16[208,256]{1,0:T(8,128)(2,1)S(1)}, u32[]{:S(2)}, u32[]{:S(2)}) collective-permute-start(bf16[208,256]{1,0:T(8,128)(2,1)S(1)} %get-tuple-element.22), channel_id=1, source_target_pairs={{0,4},{4,0},{8,12},{12,8},{16,20},{20,16},{24,28},{28,24},{1,5},{5... | collective-permute-start | bytes 319496 | tf_op jit(solution)/shard_map/ppermute | solution.py:247
  13.1 1.9 %collective-permute-start.4 = (bf16[208,256]{1,0:T(8,128)(2,1)S(1)}, bf16[208,256]{1,0:T(8,128)(2,1)S(1)}, u32[]{:S(2)}, u32[]{:S(2)}) collective-permute-start(bf16[208,256]{1,0:T(8,128)(2,1)S(1)} %get-tuple-element.23), channel_id=1, source_target_pairs={{0,8},{4,12},{8,0},{12,4},{16,24},{20,28},{24,16},{28,20},{1,9},{5... | collective-permute-start | bytes 319496 | tf_op jit(solution)/shard_map/ppermute | solution.py:247
  15.1 1.5 %collective-permute-start = (bf16[208,256]{1,0:T(8,128)(2,1)S(1)}, bf16[208,256]{1,0:T(8,128)(2,1)S(1)}, u32[]{:S(2)}, u32[]{:S(2)}) collective-permute-start(bf16[208,256]{1,0:T(8,128)(2,1)S(1)} %get-tuple-element.18), channel_id=1, source_target_pairs={{0,4},{4,0},{8,12},{12,8},{16,20},{20,16},{24,28},{28,24},{1,5},{5... | collective-permute-start | bytes 319496 | tf_op jit(solution)/shard_map/ppermute | solution.py:247
  16.6 1.9 %collective-permute-start.1 = (bf16[208,256]{1,0:T(8,128)(2,1)S(1)}, bf16[208,256]{1,0:T(8,128)(2,1)S(1)}, u32[]{:S(2)}, u32[]{:S(2)}) collective-permute-start(bf16[208,256]{1,0:T(8,128)(2,1)S(1)} %get-tuple-element.19), channel_id=1, source_target_pairs={{0,8},{4,12},{8,0},{12,4},{16,24},{20,28},{24,16},{28,20},{1,9},{5... | collective-permute-start | bytes 319496 | tf_op jit(solution)/shard_map/ppermute | solution.py:247
  18.6 0.7 %collective-permute-start.2 = (bf16[208,256]{1,0:T(8,128)(2,1)S(1)}, bf16[208,256]{1,0:T(8,128)(2,1)S(1)}, u32[]{:S(2)}, u32[]{:S(2)}) collective-permute-start(bf16[208,256]{1,0:T(8,128)(2,1)S(1)} %get-tuple-element.20), channel_id=1, source_target_pairs={{0,12},{4,8},{8,4},{12,0},{16,28},{20,24},{24,20},{28,16},{1,13},{... | collective-permute-start | bytes 319496 | tf_op jit(solution)/shard_map/ppermute | solution.py:247
  19.2 2.7 %collective-permute-done.5.refs_3_ = bf16[208,256]{1,0:T(8,128)(2,1)S(1)} collective-permute-done((bf16[208,256]{1,0:T(8,128)(2,1)S(1)}, bf16[208,256]{1,0:T(8,128)(2,1)S(1)}, u32[]{:S(2)}, u32[]{:S(2)}) %collective-permute-start.5) | collective-permute-done | bytes 106528 | tf_op jit(solution)/shard_map/ppermute | solution.py:247
  22.4 2.5 %collective-permute-start.6 = (bf16[208,256]{1,0:T(8,128)(2,1)S(1)}, bf16[208,256]{1,0:T(8,128)(2,1)S(1)}, u32[]{:S(2)}, u32[]{:S(2)}) collective-permute-start(bf16[208,256]{1,0:T(8,128)(2,1)S(1)} %shard_map.74), channel_id=1, source_target_pairs={{0,16},{4,20},{8,24},{12,28},{16,0},{20,4},{24,8},{28,12},{1,17},{... | collective-permute-start | bytes 319496 | tf_op jit(solution)/shard_map/ppermute | solution.py:247
  24.9 1.0 %collective-permute-done.2.refs_3_ = bf16[208,256]{1,0:T(8,128)(2,1)S(1)} collective-permute-done((bf16[208,256]{1,0:T(8,128)(2,1)S(1)}, bf16[208,256]{1,0:T(8,128)(2,1)S(1)}, u32[]{:S(2)}, u32[]{:S(2)}) %collective-permute-start.2) | collective-permute-done | bytes 106528 | tf_op jit(solution)/shard_map/ppermute | solution.py:247
  25.9 3.7 %collective-permute-done.6.refs_4_ = bf16[208,256]{1,0:T(8,128)(2,1)S(1)} collective-permute-done((bf16[208,256]{1,0:T(8,128)(2,1)S(1)}, bf16[208,256]{1,0:T(8,128)(2,1)S(1)}, u32[]{:S(2)}, u32[]{:S(2)}) %collective-permute-start.6) | collective-permute-done | bytes 106528 | tf_op jit(solution)/shard_map/ppermute | solution.py:247
  30.1 1.0 %collective-permute-start.11 = (bf16[192,256]{1,0:T(8,128)(2,1)S(1)}, bf16[192,256]{1,0:T(8,128)(2,1)S(1)}, u32[]{:S(2)}, u32[]{:S(2)}) collective-permute-start(bf16[192,256]{1,0:T(8,128)(2,1)S(1)} %shard_map.75.refs_0_), channel_id=1, source_target_pairs={{0,16},{4,20},{8,24},{12,28},{16,0},{20,4},{24,8},{28,12},{1,17},{... | collective-permute-start | bytes 294920 | tf_op jit(solution)/shard_map/ppermute | solution.py:247
  31.1 1.6 %collective-permute-start.10 = (bf16[192,256]{1,0:T(8,128)(2,1)S(1)}, bf16[192,256]{1,0:T(8,128)(2,1)S(1)}, u32[]{:S(2)}, u32[]{:S(2)}) collective-permute-start(bf16[192,256]{1,0:T(8,128)(2,1)S(1)} %shard_map.75.refs_0_), channel_id=1, source_target_pairs={{0,24},{4,28},{8,16},{12,20},{16,8},{20,12},{24,0},{28,4},{1,25},{... | collective-permute-start | bytes 294920 | tf_op jit(solution)/shard_map/ppermute | solution.py:247
  32.7 1.0 %collective-permute-start.7 = (bf16[192,256]{1,0:T(8,128)(2,1)S(1)}, bf16[192,256]{1,0:T(8,128)(2,1)S(1)}, u32[]{:S(2)}, u32[]{:S(2)}) collective-permute-start(bf16[192,256]{1,0:T(8,128)(2,1)S(1)} %shard_map.75.refs_0_), channel_id=1, source_target_pairs={{0,12},{4,8},{8,4},{12,0},{16,28},{20,24},{24,20},{28,16},{1,13},{... | collective-permute-start | bytes 294920 | tf_op jit(solution)/shard_map/ppermute | solution.py:247
  33.8 1.5 %collective-permute-start.8 = (bf16[192,256]{1,0:T(8,128)(2,1)S(1)}, bf16[192,256]{1,0:T(8,128)(2,1)S(1)}, u32[]{:S(2)}, u32[]{:S(2)}) collective-permute-start(bf16[192,256]{1,0:T(8,128)(2,1)S(1)} %shard_map.75.refs_0_), channel_id=1, source_target_pairs={{0,8},{4,12},{8,0},{12,4},{16,24},{20,28},{24,16},{28,20},{1,9},{5... | collective-permute-start | bytes 294920 | tf_op jit(solution)/shard_map/ppermute | solution.py:247
  35.3 0.9 %collective-permute-start.9 = (bf16[192,256]{1,0:T(8,128)(2,1)S(1)}, bf16[192,256]{1,0:T(8,128)(2,1)S(1)}, u32[]{:S(2)}, u32[]{:S(2)}) collective-permute-start(bf16[192,256]{1,0:T(8,128)(2,1)S(1)} %shard_map.75.refs_0_), channel_id=1, source_target_pairs={{0,4},{4,0},{8,12},{12,8},{16,20},{20,16},{24,28},{28,24},{1,5},{5... | collective-permute-start | bytes 294920 | tf_op jit(solution)/shard_map/ppermute | solution.py:247
  36.6 0.8 %collective-permute-start.12 = (bf16[192,256]{1,0:T(8,128)(2,1)S(1)}, bf16[192,256]{1,0:T(8,128)(2,1)S(1)}, u32[]{:S(2)}, u32[]{:S(2)}) collective-permute-start(bf16[192,256]{1,0:T(8,128)(2,1)S(1)} %collective-permute-done.11.refs_5_), channel_id=1, source_target_pairs={{0,4},{4,0},{8,12},{12,8},{16,20},{20,16},{24,28},{28,24},{1,5},{5... | collective-permute-start | bytes 294920 | tf_op jit(solution)/shard_map/ppermute | solution.py:247
  37.3 0.9 %collective-permute-done.10.refs_4_ = bf16[192,256]{1,0:T(8,128)(2,1)S(1)} collective-permute-done((bf16[192,256]{1,0:T(8,128)(2,1)S(1)}, bf16[192,256]{1,0:T(8,128)(2,1)S(1)}, u32[]{:S(2)}, u32[]{:S(2)}) %collective-permute-start.10) | collective-permute-done | bytes 98336 | tf_op jit(solution)/shard_map/ppermute | solution.py:247
  38.3 0.7 %collective-permute-start.13 = (bf16[192,256]{1,0:T(8,128)(2,1)S(1)}, bf16[192,256]{1,0:T(8,128)(2,1)S(1)}, u32[]{:S(2)}, u32[]{:S(2)}) collective-permute-start(bf16[192,256]{1,0:T(8,128)(2,1)S(1)} %collective-permute-done.10.refs_4_), channel_id=1, source_target_pairs={{0,4},{4,0},{8,12},{12,8},{16,20},{20,16},{24,28},{28,24},{1,5},{5... | collective-permute-start | bytes 294920 | tf_op jit(solution)/shard_map/ppermute | solution.py:247
  40.7 0.8 %shard_map.76.refs_0_ = f32[192,1024]{1,0:T(8,128)S(1)} custom-call(bf16[192,256]{1,0:T(8,128)(2,1)S(1)} %shard_map.75.refs_0_, bf16[192,256]{1,0:T(8,128)(2,1)S(1)} %collective-permute-done.7.refs_1_, bf16[192,256]{1,0:T(8,128)(2,1)S(1)} %collective-permute-done.8.refs_2_, bf16[192,256]{1,0:T(8,128)(2,1)S(1)} %collective-permute-done.9.refs_3_, ...), custom_call_target="tpu_custom_call" | custom-call | flops 603979776 | bytes 3145728 | tf_op jit(solution)/shard_map/pallas_call | solution.py:329
  41.7 1.1 %collective-permute-done.13.refs_2_ = bf16[192,256]{1,0:T(8,128)(2,1)S(1)} collective-permute-done((bf16[192,256]{1,0:T(8,128)(2,1)S(1)}, bf16[192,256]{1,0:T(8,128)(2,1)S(1)}, u32[]{:S(2)}, u32[]{:S(2)}) %collective-permute-start.13) | collective-permute-done | bytes 98336 | tf_op jit(solution)/shard_map/ppermute | solution.py:247
  43.4 1.6 %collective-permute-start.15 = (bf16[48,1024]{1,0:T(8,128)(2,1)S(1)}, bf16[48,1024]{1,0:T(8,128)(2,1)S(1)}, u32[]{:S(2)}, u32[]{:S(2)}) collective-permute-start(bf16[48,1024]{1,0:T(8,128)(2,1)S(1)} %get-tuple-element.27), channel_id=1, source_target_pairs={{0,2},{1,3},{2,0},{3,1},{4,6},{5,7},{6,4},{7,5},{8,10},{9,11},{10,... | collective-permute-start | bytes 294920 | tf_op jit(solution)/shard_map/ppermute | solution.py:247
  45.3 3.8 %collective-permute-done.15 = bf16[48,1024]{1,0:T(8,128)(2,1)S(1)} collective-permute-done((bf16[48,1024]{1,0:T(8,128)(2,1)S(1)}, bf16[48,1024]{1,0:T(8,128)(2,1)S(1)}, u32[]{:S(2)}, u32[]{:S(2)}) %collective-permute-start.15) | collective-permute-done | bytes 98336 | tf_op jit(solution)/shard_map/ppermute | solution.py:247
  49.1 1.2 %collective-permute-done.16 = bf16[48,1024]{1,0:T(8,128)(2,1)S(1)} collective-permute-done((bf16[48,1024]{1,0:T(8,128)(2,1)S(1)}, bf16[48,1024]{1,0:T(8,128)(2,1)S(1)}, u32[]{:S(2)}, u32[]{:S(2)}) %collective-permute-start.16) | collective-permute-done | bytes 98336 | tf_op jit(solution)/shard_map/ppermute | solution.py:247
  50.3 0.7 %add_convert_fusion = bf16[48,1024]{1,0:T(8,128)(2,1)} fusion(bf16[48,1024]{1,0:T(8,128)(2,1)S(1)} %collective-permute-done.16, bf16[48,1024]{1,0:T(8,128)(2,1)S(1)} %collective-permute-done.15, bf16[48,1024]{1,0:T(8,128)(2,1)S(1)} %collective-permute-done.14, bf16[48,1024]{1,0:T(8,128)(2,1)S(1)} %get-tuple-element.25), kind=kLoop, calls=%fused_computation | loop fusion | flops 393216 | bytes 491520 | tf_op jit(solution)/shard_map/convert_element_type | solution.py:350
  (18 shorter events, 4.0 us)
Async XLA Ops:
  0.0 40.7 %copy-start = (bf16[2048,1024]{1,0:T(8,128)(2,1)S(1)}, bf16[2048,1024]{1,0:T(8,128)(2,1)}, u32[]{:S(2)}) copy-start(bf16[2048,1024]{1,0:T(8,128)(2,1)} %refs_3_.1) | copy-start | bytes 12582916
  10.0 8.6 %collective-permute-start.3 = (bf16[208,256]{1,0:T(8,128)(2,1)S(1)}, bf16[208,256]{1,0:T(8,128)(2,1)S(1)}, u32[]{:S(2)}, u32[]{:S(2)}) collective-permute-start(bf16[208,256]{1,0:T(8,128)(2,1)S(1)} %get-tuple-element.22), channel_id=1, source_target_pairs={{0,4},{4,0},{8,12},{12,8},{16,20},{20,16},{24,28},{28,24},{1,5},{5... | collective-permute-start | bytes 319496 | tf_op jit(solution)/shard_map/ppermute | solution.py:247
  13.1 6.1 %collective-permute-start.4 = (bf16[208,256]{1,0:T(8,128)(2,1)S(1)}, bf16[208,256]{1,0:T(8,128)(2,1)S(1)}, u32[]{:S(2)}, u32[]{:S(2)}) collective-permute-start(bf16[208,256]{1,0:T(8,128)(2,1)S(1)} %get-tuple-element.23), channel_id=1, source_target_pairs={{0,8},{4,12},{8,0},{12,4},{16,24},{20,28},{24,16},{28,20},{1,9},{5... | collective-permute-start | bytes 319496 | tf_op jit(solution)/shard_map/ppermute | solution.py:247
  15.1 6.9 %collective-permute-start.5 = (bf16[208,256]{1,0:T(8,128)(2,1)S(1)}, bf16[208,256]{1,0:T(8,128)(2,1)S(1)}, u32[]{:S(2)}, u32[]{:S(2)}) collective-permute-start(bf16[208,256]{1,0:T(8,128)(2,1)S(1)} %get-tuple-element.24), channel_id=1, source_target_pairs={{0,12},{4,8},{8,4},{12,0},{16,28},{20,24},{24,20},{28,16},{1,13},{... | collective-permute-start | bytes 319496 | tf_op jit(solution)/shard_map/ppermute | solution.py:247
  15.1 9.8 %collective-permute-start = (bf16[208,256]{1,0:T(8,128)(2,1)S(1)}, bf16[208,256]{1,0:T(8,128)(2,1)S(1)}, u32[]{:S(2)}, u32[]{:S(2)}) collective-permute-start(bf16[208,256]{1,0:T(8,128)(2,1)S(1)} %get-tuple-element.18), channel_id=1, source_target_pairs={{0,4},{4,0},{8,12},{12,8},{16,20},{20,16},{24,28},{28,24},{1,5},{5... | collective-permute-start | bytes 319496 | tf_op jit(solution)/shard_map/ppermute | solution.py:247
  16.6 8.3 %collective-permute-start.1 = (bf16[208,256]{1,0:T(8,128)(2,1)S(1)}, bf16[208,256]{1,0:T(8,128)(2,1)S(1)}, u32[]{:S(2)}, u32[]{:S(2)}) collective-permute-start(bf16[208,256]{1,0:T(8,128)(2,1)S(1)} %get-tuple-element.19), channel_id=1, source_target_pairs={{0,8},{4,12},{8,0},{12,4},{16,24},{20,28},{24,16},{28,20},{1,9},{5... | collective-permute-start | bytes 319496 | tf_op jit(solution)/shard_map/ppermute | solution.py:247
  18.6 7.4 %collective-permute-start.2 = (bf16[208,256]{1,0:T(8,128)(2,1)S(1)}, bf16[208,256]{1,0:T(8,128)(2,1)S(1)}, u32[]{:S(2)}, u32[]{:S(2)}) collective-permute-start(bf16[208,256]{1,0:T(8,128)(2,1)S(1)} %get-tuple-element.20), channel_id=1, source_target_pairs={{0,12},{4,8},{8,4},{12,0},{16,28},{20,24},{24,20},{28,16},{1,13},{... | collective-permute-start | bytes 319496 | tf_op jit(solution)/shard_map/ppermute | solution.py:247
  22.4 7.2 %collective-permute-start.6 = (bf16[208,256]{1,0:T(8,128)(2,1)S(1)}, bf16[208,256]{1,0:T(8,128)(2,1)S(1)}, u32[]{:S(2)}, u32[]{:S(2)}) collective-permute-start(bf16[208,256]{1,0:T(8,128)(2,1)S(1)} %shard_map.74), channel_id=1, source_target_pairs={{0,16},{4,20},{8,24},{12,28},{16,0},{20,4},{24,8},{28,12},{1,17},{... | collective-permute-start | bytes 319496 | tf_op jit(solution)/shard_map/ppermute | solution.py:247
  30.1 6.5 %collective-permute-start.11 = (bf16[192,256]{1,0:T(8,128)(2,1)S(1)}, bf16[192,256]{1,0:T(8,128)(2,1)S(1)}, u32[]{:S(2)}, u32[]{:S(2)}) collective-permute-start(bf16[192,256]{1,0:T(8,128)(2,1)S(1)} %shard_map.75.refs_0_), channel_id=1, source_target_pairs={{0,16},{4,20},{8,24},{12,28},{16,0},{20,4},{24,8},{28,12},{1,17},{... | collective-permute-start | bytes 294920 | tf_op jit(solution)/shard_map/ppermute | solution.py:247
  31.1 7.2 %collective-permute-start.10 = (bf16[192,256]{1,0:T(8,128)(2,1)S(1)}, bf16[192,256]{1,0:T(8,128)(2,1)S(1)}, u32[]{:S(2)}, u32[]{:S(2)}) collective-permute-start(bf16[192,256]{1,0:T(8,128)(2,1)S(1)} %shard_map.75.refs_0_), channel_id=1, source_target_pairs={{0,24},{4,28},{8,16},{12,20},{16,8},{20,12},{24,0},{28,4},{1,25},{... | collective-permute-start | bytes 294920 | tf_op jit(solution)/shard_map/ppermute | solution.py:247
  32.7 6.8 %collective-permute-start.7 = (bf16[192,256]{1,0:T(8,128)(2,1)S(1)}, bf16[192,256]{1,0:T(8,128)(2,1)S(1)}, u32[]{:S(2)}, u32[]{:S(2)}) collective-permute-start(bf16[192,256]{1,0:T(8,128)(2,1)S(1)} %shard_map.75.refs_0_), channel_id=1, source_target_pairs={{0,12},{4,8},{8,4},{12,0},{16,28},{20,24},{24,20},{28,16},{1,13},{... | collective-permute-start | bytes 294920 | tf_op jit(solution)/shard_map/ppermute | solution.py:247
  33.8 6.4 %collective-permute-start.8 = (bf16[192,256]{1,0:T(8,128)(2,1)S(1)}, bf16[192,256]{1,0:T(8,128)(2,1)S(1)}, u32[]{:S(2)}, u32[]{:S(2)}) collective-permute-start(bf16[192,256]{1,0:T(8,128)(2,1)S(1)} %shard_map.75.refs_0_), channel_id=1, source_target_pairs={{0,8},{4,12},{8,0},{12,4},{16,24},{20,28},{24,16},{28,20},{1,9},{5... | collective-permute-start | bytes 294920 | tf_op jit(solution)/shard_map/ppermute | solution.py:247
  35.3 5.4 %collective-permute-start.9 = (bf16[192,256]{1,0:T(8,128)(2,1)S(1)}, bf16[192,256]{1,0:T(8,128)(2,1)S(1)}, u32[]{:S(2)}, u32[]{:S(2)}) collective-permute-start(bf16[192,256]{1,0:T(8,128)(2,1)S(1)} %shard_map.75.refs_0_), channel_id=1, source_target_pairs={{0,4},{4,0},{8,12},{12,8},{16,20},{20,16},{24,28},{28,24},{1,5},{5... | collective-permute-start | bytes 294920 | tf_op jit(solution)/shard_map/ppermute | solution.py:247
  36.6 5.2 %collective-permute-start.12 = (bf16[192,256]{1,0:T(8,128)(2,1)S(1)}, bf16[192,256]{1,0:T(8,128)(2,1)S(1)}, u32[]{:S(2)}, u32[]{:S(2)}) collective-permute-start(bf16[192,256]{1,0:T(8,128)(2,1)S(1)} %collective-permute-done.11.refs_5_), channel_id=1, source_target_pairs={{0,4},{4,0},{8,12},{12,8},{16,20},{20,16},{24,28},{28,24},{1,5},{5... | collective-permute-start | bytes 294920 | tf_op jit(solution)/shard_map/ppermute | solution.py:247
  38.3 4.6 %collective-permute-start.13 = (bf16[192,256]{1,0:T(8,128)(2,1)S(1)}, bf16[192,256]{1,0:T(8,128)(2,1)S(1)}, u32[]{:S(2)}, u32[]{:S(2)}) collective-permute-start(bf16[192,256]{1,0:T(8,128)(2,1)S(1)} %collective-permute-done.10.refs_4_), channel_id=1, source_target_pairs={{0,4},{4,0},{8,12},{12,8},{16,20},{20,16},{24,28},{28,24},{1,5},{5... | collective-permute-start | bytes 294920 | tf_op jit(solution)/shard_map/ppermute | solution.py:247
  43.3 1.9 %collective-permute-start.14 = (bf16[48,1024]{1,0:T(8,128)(2,1)S(1)}, bf16[48,1024]{1,0:T(8,128)(2,1)S(1)}, u32[]{:S(2)}, u32[]{:S(2)}) collective-permute-start(bf16[48,1024]{1,0:T(8,128)(2,1)S(1)} %get-tuple-element.26), channel_id=1, source_target_pairs={{0,1},{1,0},{2,3},{3,2},{4,5},{5,4},{6,7},{7,6},{8,9},{9,8},{10,11... | collective-permute-start | bytes 294920 | tf_op jit(solution)/shard_map/ppermute | solution.py:247
  43.4 5.7 %collective-permute-start.15 = (bf16[48,1024]{1,0:T(8,128)(2,1)S(1)}, bf16[48,1024]{1,0:T(8,128)(2,1)S(1)}, u32[]{:S(2)}, u32[]{:S(2)}) collective-permute-start(bf16[48,1024]{1,0:T(8,128)(2,1)S(1)} %get-tuple-element.27), channel_id=1, source_target_pairs={{0,2},{1,3},{2,0},{3,1},{4,6},{5,7},{6,4},{7,5},{8,10},{9,11},{10,... | collective-permute-start | bytes 294920 | tf_op jit(solution)/shard_map/ppermute | solution.py:247
  45.0 5.3 %collective-permute-start.16 = (bf16[48,1024]{1,0:T(8,128)(2,1)S(1)}, bf16[48,1024]{1,0:T(8,128)(2,1)S(1)}, u32[]{:S(2)}, u32[]{:S(2)}) collective-permute-start(bf16[48,1024]{1,0:T(8,128)(2,1)S(1)} %get-tuple-element.28), channel_id=1, source_target_pairs={{0,3},{1,2},{2,1},{3,0},{4,7},{5,6},{6,5},{7,4},{8,11},{9,10},{10,... | collective-permute-start | bytes 294920 | tf_op jit(solution)/shard_map/ppermute | solution.py:247
